TPU v7x, 32 devices: a whole 2x2x4 slice. The times are simulated.
32 devices in a mesh: pipe: 2 (over x), dp: 4 (over z), row: 2 (over core), col: 2 (over y).
Axes of the slice: x: 2, y: 2, z: 4, core: 2. Of those that a mesh axis runs over, the one named last changes fastest.
Arguments:
- images: bfloat16 [16, 196, 512], P(('dp', 'row'), 'col'), may hold values from -6 to 6
- extents: int32 [16, 2], P(('dp', 'row')), may hold values from 8 to 14
- cotangent: bfloat16 [16, 196, 512], P(('dp', 'row'), 'col'), may hold values from -6 to 6
- qkv_weight: bfloat16 [2, 512, 3, 512], P('pipe', 'row', None, 'col'), may hold values from -0.25 to 0.25
- qkv_bias: float32 [2, 2, 512], P('pipe', None, 'col'), may hold values from -3 to 3
- proj_weight: bfloat16 [2, 512, 512], P('pipe', 'col', 'row'), may hold values from -1 to 1
- proj_bias: float32 [2, 512], P('pipe'), may hold values from -3 to 3
- fc1_weight: bfloat16 [2, 512, 2048], P('pipe', 'row', 'col'), may hold values from -0.25 to 0.25
- fc1_bias: float32 [2, 2048], P('pipe', 'col'), may hold values from -3 to 3
- fc2_weight: bfloat16 [2, 2048, 512], P('pipe', 'col', 'row'), may hold values from -0.125 to 0.125
- fc2_bias: float32 [2, 512], P('pipe'), may hold values from -3 to 3
- norm_gain: float32 [2, 2, 512], P('pipe'), may hold values from 0.5 to 1.5
- norm_bias: float32 [2, 2, 512], P('pipe'), may hold values from -3 to 3
- bias_table: float32 [2, 169, 16], P('pipe', None, 'col'), may hold values from -5 to 5
Outputs:
- layer_outputs: bfloat16 [2, 16, 196, 512], P('pipe', ('dp', 'row'), 'col')
- input_grads: bfloat16 [2, 16, 196, 512], P('pipe', ('dp', 'row'), 'col')
- qkv_weight_grad: float32 [2, 512, 3, 512], P('pipe', 'row', None, 'col')
- qkv_bias_grad: float32 [2, 2, 512], P('pipe', None, 'col')
- proj_weight_grad: float32 [2, 512, 512], P('pipe', 'col', 'row')
- proj_bias_grad: float32 [2, 512], P('pipe')
- fc1_weight_grad: float32 [2, 512, 2048], P('pipe', 'row', 'col')
- fc1_bias_grad: float32 [2, 2048], P('pipe', 'col')
- fc2_weight_grad: float32 [2, 2048, 512], P('pipe', 'col', 'row')
- fc2_bias_grad: float32 [2, 512], P('pipe')
- norm_gain_grad: float32 [2, 2, 512], P('pipe')
- norm_bias_grad: float32 [2, 2, 512], P('pipe')
- table_grad: float32 [2, 169, 16], P('pipe', None, 'col')
All inputs are finite; a program needn't handle non-finite values.
Results may differ from a plain program's by a relative error of at most 0.022.
Values may be sent and summed in bfloat16 or wider, within the bound.
A program may use at most 128 MiB of HBM per device.

v0:
```python
import jax
import jax.numpy as jnp
from jax import lax
from jax.sharding import PartitionSpec as P

HEAD_DIM = 32
WINDOW = 7
SIDE = 14
SHIFT = 3
SPAN = 13
TABLE = 169
MICRO = 2


exact_precision = lax.Precision.HIGHEST
blocked_value = -1000000000.0


def shifted(x, axis, by):
    size = lax.axis_size(axis)
    pairs = [(i, i + by) for i in range(size) if 0 <= i + by < size]
    return lax.ppermute(x, axis, pairs)


def layer_norm(values, gain, offset):
    row_mean = jnp.mean(values, -1, keepdims=True)
    centred = values - row_mean
    variance = jnp.mean(centred * centred, -1, keepdims=True)
    return centred * lax.rsqrt(variance + 1e-05) * gain + offset


def exact_gelu(values):
    return jax.nn.gelu(values, approximate=False)


def to_windows(token_rows, offset_cells):
    image_count = token_rows.shape[0]
    features = token_rows.shape[-1]
    cell_grid = token_rows.reshape(image_count, SIDE, SIDE, features)
    cell_grid = jnp.roll(cell_grid, -offset_cells, axis=1)
    cell_grid = jnp.roll(cell_grid, -offset_cells, axis=2)
    cell_grid = cell_grid.reshape(
        image_count, SIDE // WINDOW, WINDOW, SIDE // WINDOW, WINDOW, features
    )
    cell_grid = cell_grid.transpose(0, 1, 3, 2, 4, 5)
    return cell_grid.reshape(image_count * (SIDE // WINDOW) ** 2, WINDOW * WINDOW, features)


def from_windows(window_rows, offset_cells, image_count):
    features = window_rows.shape[-1]
    cell_grid = window_rows.reshape(
        image_count, SIDE // WINDOW, SIDE // WINDOW, WINDOW, WINDOW, features
    )
    cell_grid = cell_grid.transpose(0, 1, 3, 2, 4, 5).reshape(image_count, SIDE, SIDE, features)
    cell_grid = jnp.roll(cell_grid, offset_cells, axis=1)
    cell_grid = jnp.roll(cell_grid, offset_cells, axis=2)
    return cell_grid.reshape(image_count, SIDE * SIDE, features)


def window_allowed(extents, shift_flag):
    places = jnp.arange(SIDE, dtype=jnp.int32)
    source = (places + SHIFT * shift_flag) % SIDE
    padded = (source[None, :, None] >= extents[:, 0, None, None]) | (
        source[None, None, :] >= extents[:, 1, None, None]
    )
    band_index = (places >= SIDE - WINDOW).astype(jnp.int32) + (places >= SIDE - SHIFT).astype(
        jnp.int32
    )
    region_codes = (band_index[:, None] * 3 + band_index[None, :]) * shift_flag * 2 + padded.astype(
        jnp.int32
    )
    image_count = extents.shape[0]
    region_codes = region_codes.reshape(
        image_count, SIDE // WINDOW, WINDOW, SIDE // WINDOW, WINDOW
    ).transpose(0, 1, 3, 2, 4)
    region_codes = region_codes.reshape(image_count * (SIDE // WINDOW) ** 2, WINDOW * WINDOW)
    return region_codes[:, :, None] == region_codes[:, None, :]


def relative_index():
    window_cells = jnp.arange(WINDOW * WINDOW, dtype=jnp.int32)
    cell_rows = window_cells // WINDOW
    cell_cols = window_cells % WINDOW
    return (
        (cell_rows[:, None] - cell_rows[None, :] + WINDOW - 1) * SPAN
        + cell_cols[:, None]
        - cell_cols[None, :]
        + WINDOW
        - 1
    )


def gather_tokens(values):
    return lax.all_gather(values, "col", axis=1, tiled=True)


def sum_tokens(values):
    return lax.psum_scatter(
        values.astype(jnp.bfloat16), "col", scatter_dimension=1, tiled=True
    ).astype(jnp.float32)


def gather_grads(values):
    return lax.all_gather(values, "col", axis=1, tiled=True)


def sum_grads(values):
    return lax.psum_scatter(
        values.astype(jnp.bfloat16), "col", scatter_dimension=1, tiled=True
    ).astype(jnp.float32)


def attention_parts(normed, allowed, qkv_full, qkv_shift, rel_bias, offset_cells):
    windows = to_windows(normed, offset_cells)
    win_count = windows.shape[0]
    window_cells = windows.shape[1]
    local_heads = rel_bias.shape[1]
    qkv_terms = jnp.einsum("wtd,dce->wtce", windows, qkv_full, preferred_element_type=jnp.float32)
    qkv_low = (qkv_terms + qkv_shift).astype(jnp.bfloat16)
    head_split = qkv_low.reshape(win_count, window_cells, 3, local_heads, HEAD_DIM)
    query_heads = head_split[:, :, 0]
    key_heads = head_split[:, :, 1]
    value_heads = head_split[:, :, 2]
    scores = (
        HEAD_DIM ** (-0.5)
        * jnp.einsum("wqhd,wkhd->wqhk", query_heads, key_heads, preferred_element_type=jnp.float32)
        + rel_bias
    )
    scores = jnp.where(allowed[:, :, None, :], scores, blocked_value)
    top_score = jnp.max(scores, axis=-1, keepdims=True)
    weights_exp = jnp.exp(scores - top_score)
    attn_probs = weights_exp / jnp.sum(weights_exp, axis=-1, keepdims=True)
    probs_low = attn_probs.astype(jnp.bfloat16)
    mixed_heads = jnp.einsum(
        "wqhk,wkhd->wqhd", probs_low, value_heads, preferred_element_type=jnp.float32
    )
    mixed_low = mixed_heads.reshape(win_count, window_cells, local_heads * HEAD_DIM).astype(
        jnp.bfloat16
    )
    return (windows, query_heads, key_heads, value_heads, attn_probs, probs_low, mixed_low)


def forward_layer(hidden_in, allowed, weights, smalls, rel_bias, offset_cells):
    qkv_full, proj_full, fc1_full, fc2_full = weights
    norm_gains, offsets, qkv_shift, proj_shift, fc1_shift, fc2_shift = smalls
    normed = gather_tokens(layer_norm(hidden_in, norm_gains[0], offsets[0]).astype(jnp.bfloat16))
    image_count = normed.shape[0]
    parts = attention_parts(normed, allowed, qkv_full, qkv_shift, rel_bias, offset_cells)
    mixed_low = parts[6]
    attn_part = jnp.einsum("wte,ef->wtf", mixed_low, proj_full, preferred_element_type=jnp.float32)
    middle = hidden_in + (
        sum_tokens(from_windows(attn_part, offset_cells, image_count)) + proj_shift
    )
    normed_two = gather_tokens(layer_norm(middle, norm_gains[1], offsets[1]).astype(jnp.bfloat16))
    pre_act = (
        jnp.einsum("ntd,df->ntf", normed_two, fc1_full, preferred_element_type=jnp.float32)
        + fc1_shift
    )
    activation = exact_gelu(pre_act).astype(jnp.bfloat16)
    branch_part = jnp.einsum(
        "ntf,fd->ntd", activation, fc2_full, preferred_element_type=jnp.float32
    )
    branch = sum_tokens(branch_part) + fc2_shift
    return (normed, normed_two, middle, middle + branch)


def backward_layer(
    out_grad,
    hidden_in,
    middle,
    normed,
    normed_two,
    allowed,
    weights,
    smalls,
    rel_bias,
    onehot,
    offset_cells,
):
    qkv_full, proj_full, fc1_full, fc2_full = weights
    norm_gains, offsets, qkv_shift, proj_shift, fc1_shift, fc2_shift = smalls
    image_count = normed.shape[0]
    windows, query_heads, key_heads, value_heads, attn_probs, probs_low, mixed_low = (
        attention_parts(normed, allowed, qkv_full, qkv_shift, rel_bias, offset_cells)
    )
    win_count = windows.shape[0]
    window_cells = windows.shape[1]
    local_heads = rel_bias.shape[1]
    pre_act = (
        jnp.einsum("ntd,df->ntf", normed_two, fc1_full, preferred_element_type=jnp.float32)
        + fc1_shift
    )
    activation = exact_gelu(pre_act).astype(jnp.bfloat16)
    out_low = out_grad.astype(jnp.bfloat16)
    fc2_bias_grad = jnp.sum(out_low.astype(jnp.float32), axis=(0, 1))
    branch_grad = gather_grads(out_low)
    fc2_grad = jnp.einsum(
        "ntf,ntd->fd", activation, branch_grad, preferred_element_type=jnp.float32
    )
    act_grad = jnp.einsum("ntd,fd->ntf", branch_grad, fc2_full, preferred_element_type=jnp.float32)
    _, gelu_back = jax.vjp(exact_gelu, pre_act)
    pre_grad = gelu_back(act_grad)[0].astype(jnp.bfloat16)
    fc1_bias_grad = jnp.sum(pre_grad.astype(jnp.float32), axis=(0, 1))
    fc1_grad = jnp.einsum("ntd,ntf->df", normed_two, pre_grad, preferred_element_type=jnp.float32)
    normed_two_grad = sum_grads(
        jnp.einsum("ntf,df->ntd", pre_grad, fc1_full, preferred_element_type=jnp.float32)
    )
    _, second_back = jax.vjp(layer_norm, middle, norm_gains[1], offsets[1])
    middle_norm, gain_two, offset_two = second_back(normed_two_grad)
    middle_grad = out_grad + middle_norm
    attn_low = middle_grad.astype(jnp.bfloat16)
    proj_bias_grad = jnp.sum(attn_low.astype(jnp.float32), axis=(0, 1))
    attn_grad = to_windows(gather_grads(attn_low), offset_cells)
    proj_grad = jnp.einsum("wte,wtf->ef", mixed_low, attn_grad, preferred_element_type=jnp.float32)
    mixed_grad = jnp.einsum("wtf,ef->wte", attn_grad, proj_full, preferred_element_type=jnp.float32)
    mixed_grad = mixed_grad.astype(jnp.bfloat16).reshape(
        win_count, window_cells, local_heads, HEAD_DIM
    )
    prob_grad = jnp.einsum(
        "wqhd,wkhd->wqhk", mixed_grad, value_heads, preferred_element_type=jnp.float32
    )
    value_grad = jnp.einsum(
        "wqhk,wqhd->wkhd", probs_low, mixed_grad, preferred_element_type=jnp.float32
    )
    score_grad = attn_probs * (prob_grad - jnp.sum(attn_probs * prob_grad, axis=-1, keepdims=True))
    score_low = score_grad.astype(jnp.bfloat16)
    table_term = (
        jnp.sum(score_low.astype(jnp.float32), axis=0)
        .transpose(0, 2, 1)
        .reshape(window_cells * window_cells, local_heads)
    )
    table_grad = jnp.einsum("ij,ih->jh", onehot, table_term, precision=exact_precision)
    query_grad = HEAD_DIM ** (-0.5) * jnp.einsum(
        "wqhk,wkhd->wqhd", score_low, key_heads, preferred_element_type=jnp.float32
    )
    key_grad = HEAD_DIM ** (-0.5) * jnp.einsum(
        "wqhk,wqhd->wkhd", score_low, query_heads, preferred_element_type=jnp.float32
    )
    qkv_grad_low = (
        jnp.stack([query_grad, key_grad, value_grad], 2)
        .reshape(win_count, window_cells, 3, local_heads * HEAD_DIM)
        .astype(jnp.bfloat16)
    )
    qkv_sums = jnp.sum(qkv_grad_low.astype(jnp.float32), axis=(0, 1))
    qkv_bias_grad = jnp.stack([qkv_sums[0], qkv_sums[2]], 0)
    qkv_grad = jnp.einsum(
        "wtd,wtce->dce", windows, qkv_grad_low, preferred_element_type=jnp.float32
    )
    normed_part = jnp.einsum(
        "wtce,dce->wtd", qkv_grad_low, qkv_full, preferred_element_type=jnp.float32
    )
    normed_grad = sum_grads(from_windows(normed_part, offset_cells, image_count))
    _, first_back = jax.vjp(layer_norm, hidden_in, norm_gains[0], offsets[0])
    input_norm, gain_one, offset_one = first_back(normed_grad)
    input_grad = middle_grad + input_norm
    grads = (
        jnp.stack([gain_one, gain_two], 0),
        jnp.stack([offset_one, offset_two], 0),
        qkv_grad,
        qkv_bias_grad,
        proj_grad,
        proj_bias_grad,
        fc1_grad,
        fc1_bias_grad,
        fc2_grad,
        fc2_bias_grad,
        table_grad,
    )
    return (grads, input_grad)


def per_device(
    images,
    extents,
    cotangent,
    qkv_weight,
    qkv_bias,
    proj_weight,
    proj_bias,
    fc1_weight,
    fc1_bias,
    fc2_weight,
    fc2_bias,
    norm_gain,
    norm_bias,
    bias_table,
):
    section_index = lax.axis_index("pipe")
    offset_cells = SHIFT * section_index
    per_micro = images.shape[0] // MICRO
    window_cells = WINDOW * WINDOW
    local_heads = bias_table.shape[2]
    weights = (
        lax.all_gather(qkv_weight[0], "row", axis=0, tiled=True),
        lax.all_gather(proj_weight[0], "row", axis=1, tiled=True),
        lax.all_gather(fc1_weight[0], "row", axis=0, tiled=True),
        lax.all_gather(fc2_weight[0], "row", axis=1, tiled=True),
    )
    qkv_shift = jnp.stack([qkv_bias[0, 0], jnp.zeros_like(qkv_bias[0, 0]), qkv_bias[0, 1]], 0)
    smalls = (norm_gain[0], norm_bias[0], qkv_shift, proj_bias[0], fc1_bias[0], fc2_bias[0])
    onehot = (
        (relative_index()[:, :, None] == jnp.arange(TABLE, dtype=jnp.int32))
        .astype(jnp.float32)
        .reshape(window_cells * window_cells, TABLE)
    )
    rel_bias = (
        jnp.dot(onehot, bias_table[0], precision=exact_precision)
        .reshape(window_cells, window_cells, local_heads)
        .transpose(0, 2, 1)
    )
    received = jnp.zeros((per_micro,) + images.shape[1:], jnp.bfloat16)
    kept_inputs = []
    kept_middles = []
    kept_normed = []
    kept_normed_two = []
    results = []
    for tick_index in range(MICRO + 1):
        micro_index = jnp.clip(tick_index - section_index, 0, MICRO - 1)
        own_input = lax.dynamic_slice_in_dim(images, micro_index * per_micro, per_micro, 0)
        layer_input = jnp.where(section_index == 0, own_input, received)
        allowed = window_allowed(
            lax.dynamic_slice_in_dim(extents, micro_index * per_micro, per_micro, 0), section_index
        )
        normed, normed_two, middle, result = forward_layer(
            layer_input.astype(jnp.float32), allowed, weights, smalls, rel_bias, offset_cells
        )
        result_low = result.astype(jnp.bfloat16)
        kept_inputs.append(layer_input)
        kept_middles.append(middle)
        kept_normed.append(normed)
        kept_normed_two.append(normed_two)
        results.append(result_low)
        if tick_index < MICRO:
            received = shifted(result_low, "pipe", 1)
    stacked_inputs = jnp.stack(kept_inputs, 0)
    stacked_middles = jnp.stack(kept_middles, 0)
    stacked_normed = jnp.stack(kept_normed, 0)
    stacked_normed_two = jnp.stack(kept_normed_two, 0)
    stacked_results = jnp.stack(results, 0)
    layer_outputs = jnp.where(section_index == 0, stacked_results[:MICRO], stacked_results[1:])
    layer_outputs = layer_outputs.reshape((MICRO * per_micro,) + images.shape[1:])[None]
    grad_received = jnp.zeros((per_micro,) + images.shape[1:], jnp.bfloat16)
    grad_totals = None
    grad_outputs = []
    for tick_index in range(MICRO + 1):
        micro_index = jnp.where(section_index == 0, tick_index - 1, tick_index)
        is_valid = (micro_index >= 0) & (micro_index < MICRO)
        micro_safe = jnp.clip(micro_index, 0, MICRO - 1)
        own_grad = lax.dynamic_slice_in_dim(cotangent, micro_safe * per_micro, per_micro, 0)
        out_grad = jnp.where(section_index == 0, grad_received, own_grad).astype(jnp.float32)
        out_grad = jnp.where(is_valid, out_grad, 0.0)
        forward_tick = micro_safe + section_index

        def pick_kept(stacked):
            return lax.dynamic_index_in_dim(stacked, forward_tick, 0, keepdims=False)

        allowed = window_allowed(
            lax.dynamic_slice_in_dim(extents, micro_safe * per_micro, per_micro, 0), section_index
        )
        grads, input_grad = backward_layer(
            out_grad,
            pick_kept(stacked_inputs).astype(jnp.float32),
            pick_kept(stacked_middles),
            pick_kept(stacked_normed),
            pick_kept(stacked_normed_two),
            allowed,
            weights,
            smalls,
            rel_bias,
            onehot,
            offset_cells,
        )
        grad_totals = grads if grad_totals is None else jax.tree.map(jnp.add, grad_totals, grads)
        input_low = input_grad.astype(jnp.bfloat16)
        grad_outputs.append(input_low)
        if tick_index < MICRO:
            grad_received = shifted(input_low, "pipe", -1)
    stacked_grads = jnp.stack(grad_outputs, 0)
    input_grads = jnp.where(section_index == 0, stacked_grads[1:], stacked_grads[:MICRO])
    input_grads = input_grads.reshape((MICRO * per_micro,) + images.shape[1:])[None]
    (
        gain_acc,
        offset_acc,
        qkv_acc,
        qkv_bias_acc,
        proj_acc,
        proj_bias_acc,
        fc1_acc,
        fc1_bias_acc,
        fc2_acc,
        fc2_bias_acc,
        table_acc,
    ) = grad_totals
    gain_out, offset_out, proj_bias_out, fc2_bias_out = lax.psum(
        (gain_acc, offset_acc, proj_bias_acc, fc2_bias_acc), ("dp", "row", "col")
    )
    totals = lax.psum(
        (qkv_acc, proj_acc, fc1_acc, fc2_acc, qkv_bias_acc, fc1_bias_acc, table_acc), ("dp", "row")
    )
    row_index = lax.axis_index("row")
    row_share = qkv_acc.shape[0] // lax.axis_size("row")
    qkv_out = lax.dynamic_slice_in_dim(totals[0], row_index * row_share, row_share, 0)
    proj_out = lax.dynamic_slice_in_dim(totals[1], row_index * row_share, row_share, 1)
    fc1_out = lax.dynamic_slice_in_dim(totals[2], row_index * row_share, row_share, 0)
    fc2_out = lax.dynamic_slice_in_dim(totals[3], row_index * row_share, row_share, 1)
    qkv_bias_out = totals[4]
    fc1_bias_out = totals[5]
    table_out = totals[6]
    return (
        layer_outputs,
        input_grads,
        qkv_out[None],
        qkv_bias_out[None],
        proj_out[None],
        proj_bias_out[None],
        fc1_out[None],
        fc1_bias_out[None],
        fc2_out[None],
        fc2_bias_out[None],
        gain_out[None],
        offset_out[None],
        table_out[None],
    )


def solution(mesh):
    placed = (
        P(("dp", "row"), "col", None),
        P(("dp", "row"), None),
        P(("dp", "row"), "col", None),
        P("pipe", "row", None, "col"),
        P("pipe", None, "col"),
        P("pipe", "col", "row"),
        P("pipe", None),
        P("pipe", "row", "col"),
        P("pipe", "col"),
        P("pipe", "col", "row"),
        P("pipe", None),
        P("pipe", None, None),
        P("pipe", None, None),
        P("pipe", None, "col"),
    )
    return jax.shard_map(
        per_device,
        mesh=mesh,
        in_specs=placed,
        out_specs=(
            P("pipe", ("dp", "row"), "col", None),
            P("pipe", ("dp", "row"), "col", None),
            P("pipe", "row", None, "col"),
            P("pipe", None, "col"),
            P("pipe", "col", "row"),
            P("pipe", None),
            P("pipe", "row", "col"),
            P("pipe", "col"),
            P("pipe", "col", "row"),
            P("pipe", None),
            P("pipe", None, None),
            P("pipe", None, None),
            P("pipe", None, "col"),
        ),
        check_vma=False,
    )
```

profile of v0, /device:TPU:0, one launch (start us, length us, event | category | flops | bytes accessed | tf_op | source)
XLA Modules:
  0.0 743.9 jit_solution(9754578260643799580)
XLA Ops:
  28.3 8.8 %all_gather.48 = bf16[1,196,512]{2,0,1:T(2,128)(2,1)S(1)} all-gather(bf16[1,98,512]{2,0,1:T(2,128)(2,1)S(1)} %copy.495), channel_id=1, replica_groups=mesh['pipe'=2,'dp'=4,'row'=2,'col'=2] {'col'}, dimensions={1}, use_global_device_ids=true | all-gather | bytes 301056 | tf_op jit(solution)/shard_map/all_gather | solution.py:94
  49.8 8.1 %fusion = bf16[104,512]{1,0:T(8,128)(2,1)S(1)} fusion(bf16[1,196,512]{2,1,0:T(8,128)(2,1)S(1)} %convert_element_type.653), kind=kCustom, calls=%all-reduce-scatter | all-reduce-scatter fusion | flops 106497 | bytes 307712
  60.1 11.7 %all-reduce.30.cloned.1.call-start = ((), (), s32[]{:S(2)}) async-start(), calls=%async_computation.2 | async-start | bytes 12582912 | tf_op jit(solution)/shard_map/psum | solution.py:397
  76.7 6.4 all_gather.51
  87.1 6.5 fusion.1
  106.2 6.6 all_gather.54
  127.1 9.7 %fusion.2 = bf16[104,512]{1,0:T(8,128)(2,1)S(1)} fusion(bf16[1,196,512]{2,1,0:T(8,128)(2,1)} %convert_element_type.670), kind=kCustom, calls=%all-reduce-scatter.2 | all-reduce-scatter fusion | flops 106497 | bytes 307712
  141.2 7.0 all_gather.55
  152.5 10.2 %fusion.3 = bf16[104,512]{1,0:T(8,128)(2,1)} fusion(bf16[1,196,512]{2,1,0:T(8,128)(2,1)} %fusion.76), kind=kCustom, calls=%all-reduce-scatter.3 | all-reduce-scatter fusion | flops 106497 | bytes 307712
  170.5 4.5 collective-permute-start.1
  178.2 9.8 %all_gather.58 = bf16[1,196,512]{2,0,1:T(2,128)(2,1)} all-gather(bf16[1,98,512]{2,0,1:T(2,128)(2,1)} %copy.535), channel_id=1, replica_groups=mesh['pipe'=2,'dp'=4,'row'=2,'col'=2] {'col'}, dimensions={1}, use_global_device_ids=true | all-gather | bytes 301056 | tf_op jit(solution)/shard_map/all_gather | solution.py:104
  191.8 6.6 all_gather.56
  219.5 7.0 fusion.4
  227.2 4.9 collective-permute-start.8
  268.6 7.1 all_gather.57
  287.8 7.6 %fusion.6 = bf16[104,512]{1,0:T(8,128)(2,1)} fusion(bf16[1,196,512]{2,1,0:T(8,128)(2,1)} %fusion.78), kind=kCustom, calls=%all-reduce-scatter.6 | all-reduce-scatter fusion | flops 106497 | bytes 307712
  316.9 6.9 all_gather.59
  373.2 7.6 %fusion.7 = bf16[104,512]{1,0:T(8,128)(2,1)} fusion(bf16[1,196,512]{2,1,0:T(8,128)(2,1)} %convert_element_type.708), kind=kCustom, calls=%all-reduce-scatter.7 | all-reduce-scatter fusion | flops 106497 | bytes 307712
  382.2 4.5 collective-permute-start.11
  405.8 6.6 all_gather.60
  420.4 7.6 %fusion.8 = bf16[104,512]{1,0:T(8,128)(2,1)} fusion(bf16[1,196,512]{2,1,0:T(8,128)(2,1)} %fusion.79), kind=kCustom, calls=%all-reduce-scatter.8 | all-reduce-scatter fusion | flops 106497 | bytes 307712
  428.8 4.5 collective-permute-start.12
  445.0 6.5 all_gather.61
  500.9 7.9 %fusion.9 = bf16[104,512]{1,0:T(8,128)(2,1)} fusion(bf16[1,196,512]{2,1,0:T(8,128)(2,1)} %convert_element_type.726), kind=kCustom, calls=%all-reduce-scatter.9 | all-reduce-scatter fusion | flops 106497 | bytes 307712
  510.0 4.6 collective-permute-start.13
  536.3 6.9 all_gather.62
  548.0 7.3 fusion.10
  569.2 6.6 all_gather.63
  599.7 7.6 %fusion.604 = (bf16[104,512]{1,0:T(8,128)(2,1)S(1)}, bf16[104,512]{1,0:T(8,128)(2,1)S(1)}) fusion(bf16[1,196,512]{2,1,0:T(8,128)(2,1)S(1)} %copy-done.67, bf16[1,196,512]{2,1,0:T(8,128)(2,1)S(1)} %convert_element_type.744), kind=kCustom, calls=%all-reduce-scatter.12 | all-reduce-scatter fusion | flops 212993 | bytes 614912
  612.3 28.5 %all-reduce.25 = (f32[1,2,256]{2,1,0:T(2,128)}, f32[1,1024]{1,0:T(1,128)}, f32[1,169,8]{1,2,0:T(8,128)}) all-reduce(f32[1,2,256]{2,1,0:T(2,128)S(1)} %fusion.476, f32[1,1024]{1,0:T(1,128)S(1)} %bitcast.1131, f32[1,169,8]{1,2,0:T(8,128)S(1)} %fusion.88), channel_id=1, replica_groups=mesh['pipe'=2,'dp'=4,'row'=2,'col'=2] {'dp','row'}, use_global_device_ids=true, to_apply=%region_67.72 | all-reduce | flops 2888 | bytes 23104 | tf_op jit(solution)/shard_map/psum | solution.py:397
  644.9 59.7 %all-reduce.24 = (f32[1,512]{1,0:T(1,128)}, f32[1,512]{1,0:T(1,128)}, f32[1,2,512]{2,1,0:T(2,128)}, f32[1,2,512]{2,1,0:T(2,128)}) all-reduce(f32[1,512]{1,0:T(1,128)S(1)} %bitcast.1143, f32[1,512]{1,0:T(1,128)S(1)} %bitcast.1142, f32[1,2,512]{2,1,0:T(2,128)S(1)} %fusion.472, ...), channel_id=1, replica_groups=mesh['pipe'=2,'dp'=4,'row'=2,'col'=2] {'dp','row','col'}, use_global_device_ids=true, to_apply=%region_72.77 | all-reduce | flops 3072 | bytes 24576 | tf_op jit(solution)/shard_map/psum | solution.py:394
  704.6 26.5 %all-reduce.30.cloned.1.call-done = (f32[512,3,256]{2,0,1:T(8,128)}, f32[256,512]{1,0:T(8,128)}, f32[512,1024]{1,0:T(8,128)}, f32[1024,512]{1,0:T(8,128)}) async-done(((f32[512,3,256]{2,0,1:T(8,128)}, f32[256,512]{1,0:T(8,128)}, f32[512,1024]{1,0:T(8,128)}, f32[1024,512]{1,0:T(8,128)}), (f32[512,3,256]{2,0,1:T(8,128)}, f32[256,512]{1,0:T(8,128)}, f32[512,1024]{1,0:T(8,128)}, ...) | async-done | bytes 6291472 | tf_op jit(solution)/shard_map/psum | solution.py:397
  (687 shorter events, 404.1 us)
Async XLA Ops:
  7.2 75.9 %all-gather.9.cloned.1.call-start = ((), (), s32[]{:S(2)}) async-start(), calls=%async_computation.1 | async-start | bytes 1572864 | tf_op jit(solution)/shard_map/all_gather | solution.py:297
  7.9 75.2 %all-gather.7.cloned.1.call-start = ((), (), s32[]{:S(2)}) async-start(), calls=%async_computation | async-start | bytes 1572864 | tf_op jit(solution)/shard_map/all_gather | solution.py:296
  27.8 48.7 %copy-start.75 = (f32[1,1,512]{2,1,0:T(1,128)}, f32[1,1,512]{2,1,0:T(1,128)S(1)}, u32[]{:S(2)}) copy-start(f32[1,1,512]{2,1,0:T(1,128)S(1)} %get-tuple-element.185) | copy-start | bytes 6148
  57.9 17.9 %collective-permute-start.4 = (bf16[6,512]{1,0:T(8,128)(2,1)S(1)}, bf16[6,512]{1,0:T(8,128)(2,1)S(1)}, u32[]{:S(2)}, u32[]{:S(2)}) collective-permute-start(bf16[6,512]{1,0:T(8,128)(2,1)S(1)} %slice.218), channel_id=1, source_target_pairs={{0,1},{2,3},{4,5},{6,7},{8,9},{10,11},{12,13},{14,15},{16,17},{18,... | collective-permute-start | bytes 18440
  60.1 671.0 %all-reduce.30.cloned.1.call-start = ((), (), s32[]{:S(2)}) async-start(), calls=%async_computation.2 | async-start | bytes 12582912 | tf_op jit(solution)/shard_map/psum | solution.py:397
  93.7 5.1 collective-permute-start.5
  99.7 5.9 collective-permute-start
  136.8 2.8 collective-permute-start.6
  163.4 3.3 collective-permute-start.7
  170.5 20.6 %collective-permute-start.1 = (bf16[1,98,512]{2,1,0:T(8,128)(2,1)}, bf16[1,98,512]{2,1,0:T(8,128)(2,1)S(1)}, u32[]{:S(2)}, u32[]{:S(2)}) collective-permute-start(bf16[1,98,512]{2,1,0:T(8,128)(2,1)} %get-tuple-element.167), channel_id=1, source_target_pairs={{0,16},{1,17},{2,18},{3,19},{4,20},{5,21},{6,22},{7,23},{8,24},{9,... | collective-permute-start | bytes 301064 | tf_op jit(solution)/shard_map/ppermute | solution.py:22
  227.2 39.1 %collective-permute-start.8 = (bf16[6,512]{1,0:T(8,128)(2,1)}, bf16[6,512]{1,0:T(8,128)(2,1)}, u32[]{:S(2)}, u32[]{:S(2)}) collective-permute-start(bf16[6,512]{1,0:T(8,128)(2,1)} %slice.222), channel_id=1, source_target_pairs={{0,1},{2,3},{4,5},{6,7},{8,9},{10,11},{12,13},{14,15},{16,17},{18,... | collective-permute-start | bytes 18440
  296.1 13.8 %collective-permute-start.10 = (bf16[6,512]{1,0:T(8,128)(2,1)S(1)}, bf16[6,512]{1,0:T(8,128)(2,1)S(1)}, u32[]{:S(2)}, u32[]{:S(2)}) collective-permute-start(bf16[6,512]{1,0:T(8,128)(2,1)S(1)} %slice.224), channel_id=1, source_target_pairs={{0,1},{2,3},{4,5},{6,7},{8,9},{10,11},{12,13},{14,15},{16,17},{18,... | collective-permute-start | bytes 18440
  382.2 8.0 %collective-permute-start.11 = (bf16[6,512]{1,0:T(8,128)(2,1)}, bf16[6,512]{1,0:T(8,128)(2,1)}, u32[]{:S(2)}, u32[]{:S(2)}) collective-permute-start(bf16[6,512]{1,0:T(8,128)(2,1)} %slice.225), channel_id=1, source_target_pairs={{0,1},{2,3},{4,5},{6,7},{8,9},{10,11},{12,13},{14,15},{16,17},{18,... | collective-permute-start | bytes 18440
  397.7 6.6 collective-permute-start.2
  428.8 7.4 collective-permute-start.12
  510.0 10.7 %collective-permute-start.13 = (bf16[6,512]{1,0:T(8,128)(2,1)}, bf16[6,512]{1,0:T(8,128)(2,1)}, u32[]{:S(2)}, u32[]{:S(2)}) collective-permute-start(bf16[6,512]{1,0:T(8,128)(2,1)} %slice.227), channel_id=1, source_target_pairs={{0,1},{2,3},{4,5},{6,7},{8,9},{10,11},{12,13},{14,15},{16,17},{18,... | collective-permute-start | bytes 18440
  528.3 6.6 collective-permute-start.3
  555.3 11.8 %collective-permute-start.14 = (bf16[6,512]{1,0:T(8,128)(2,1)S(1)}, bf16[6,512]{1,0:T(8,128)(2,1)S(1)}, u32[]{:S(2)}, u32[]{:S(2)}) collective-permute-start(bf16[6,512]{1,0:T(8,128)(2,1)S(1)} %slice.228), channel_id=1, source_target_pairs={{0,1},{2,3},{4,5},{6,7},{8,9},{10,11},{12,13},{14,15},{16,17},{18,... | collective-permute-start | bytes 18440
  597.1 43.9 %copy-start.85 = (f32[1,512]{1,0:T(1,128)S(1)}, f32[1,512]{1,0:T(1,128)}, u32[]{:S(2)}) copy-start(f32[1,512]{1,0:T(1,128)} %param.32) | copy-start | bytes 6148
  598.2 43.0 %copy-start.57 = (bf16[1,98,512]{2,1,0:T(8,128)(2,1)S(1)}, bf16[1,98,512]{2,1,0:T(8,128)(2,1)}, u32[]{:S(2)}) copy-start(bf16[1,98,512]{2,1,0:T(8,128)(2,1)} %copy-done.56) | copy-start | bytes 301060
  599.7 43.5 %copy-start.108 = (f32[98]{0:T(128)S(1)}, f32[98]{0:T(128)}, u32[]{:S(2)}) copy-start(f32[98]{0:T(128)} %broadcast_multiply_fusion.1) | copy-start | bytes 1180
  607.3 36.3 %copy-start.15 = (f32[1,98,512]{2,1,0:T(8,128)S(1)}, f32[1,98,512]{2,1,0:T(8,128)}, u32[]{:S(2)}) copy-start(f32[1,98,512]{2,1,0:T(8,128)} %copy-done.14) | copy-start | bytes 602116
  607.4 36.3 %copy-start.29 = (bf16[1,98,512]{2,1,0:T(8,128)(2,1)S(1)}, bf16[1,98,512]{2,1,0:T(8,128)(2,1)}, u32[]{:S(2)}) copy-start(bf16[1,98,512]{2,1,0:T(8,128)(2,1)} %get-tuple-element.136) | copy-start | bytes 301060
  607.4 36.3 %copy-start.121 = (f32[98]{0:T(128)S(1)}, f32[98]{0:T(128)}, u32[]{:S(2)}) copy-start(f32[98]{0:T(128)} %copy-done.120) | copy-start | bytes 1180
  607.4 33.4 %collective-permute-start.9 = (bf16[6,512]{1,0:T(8,128)(2,1)S(1)}, bf16[6,512]{1,0:T(8,128)(2,1)S(1)}, u32[]{:S(2)}, u32[]{:S(2)}) collective-permute-start(bf16[6,512]{1,0:T(8,128)(2,1)S(1)} %slice.223), channel_id=1, source_target_pairs={{0,1},{2,3},{4,5},{6,7},{8,9},{10,11},{12,13},{14,15},{16,17},{18,... | collective-permute-start | bytes 18440
  609.5 33.5 %collective-permute-start.15 = (bf16[6,512]{1,0:T(8,128)(2,1)S(1)}, bf16[6,512]{1,0:T(8,128)(2,1)S(1)}, u32[]{:S(2)}, u32[]{:S(2)}) collective-permute-start(bf16[6,512]{1,0:T(8,128)(2,1)S(1)} %slice.229), channel_id=1, source_target_pairs={{0,1},{2,3},{4,5},{6,7},{8,9},{10,11},{12,13},{14,15},{16,17},{18,... | collective-permute-start | bytes 18440
  610.9 32.9 %copy-start.59 = (bf16[1,98,512]{2,1,0:T(8,128)(2,1)S(1)}, bf16[1,98,512]{2,1,0:T(8,128)(2,1)}, u32[]{:S(2)}) copy-start(bf16[1,98,512]{2,1,0:T(8,128)(2,1)} %copy-done.58) | copy-start | bytes 301060
  610.9 32.9 %copy-start.61 = (bf16[1,98,512]{2,1,0:T(8,128)(2,1)S(1)}, bf16[1,98,512]{2,1,0:T(8,128)(2,1)}, u32[]{:S(2)}) copy-start(bf16[1,98,512]{2,1,0:T(8,128)(2,1)} %copy-done.60) | copy-start | bytes 301060
  612.1 32.7 %copy-start.95 = (f32[512]{0:T(512)S(1)}, f32[512]{0:T(512)}, u32[]{:S(2)}) copy-start(f32[512]{0:T(512)} %get-tuple-element.113) | copy-start | bytes 6148
  612.1 32.7 %copy-start.97 = (f32[512]{0:T(512)S(1)}, f32[512]{0:T(512)}, u32[]{:S(2)}) copy-start(f32[512]{0:T(512)} %get-tuple-element.108) | copy-start | bytes 6148
  612.2 32.7 %copy-start.99 = (f32[512]{0:T(512)S(1)}, f32[512]{0:T(512)}, u32[]{:S(2)}) copy-start(f32[512]{0:T(512)} %get-tuple-element.112) | copy-start | bytes 6148
  612.2 32.7 %copy-start.101 = (f32[512]{0:T(512)S(1)}, f32[512]{0:T(512)}, u32[]{:S(2)}) copy-start(f32[512]{0:T(512)} %get-tuple-element.109) | copy-start | bytes 6148
  (120 other events, 1302.2 us)
Sparse Core Ops, SparseCore 0:
  9.6 11.6 all-gather.8
  60.3 9.5 all-gather.6
  593.4 137.6 all-reduce.29
where the time goes:
time: 757 us; the launch traced here: 744 us
  blocking collectives  266 us (35%)
  local copies, waits for them, and re-layouts  139 us (18%)
  matrix products  133 us (18%)
  other arithmetic  90.2 us (12%)
  starting transfers between devices  61.4 us (8%)
  waiting for transfers between devices  37.5 us (5%)
  between operations  17.2 us (2%)
    unnamed x11, blocking collectives  87.2 us
    psum x1, blocking collectives, per_device(): lax.psum((gain_acc, offset_acc, proj_bias_acc, fc2_bias_acc), ('dp', 'row...  59.7 us
    all_gather x6, blocking collectives, gather_grads(): return lax.all_gather(values, 'col', axis=1, tiled=True)  43.3 us
    all_gather x6, blocking collectives, gather_tokens(): return lax.all_gather(values, 'col', axis=1, tiled=True)  42.5 us
    unnamed x12, starting transfers between devices  38.9 us
    another operation x27, local copies, waits for them, and re-layouts, backward_layer(): jnp.stack([query_grad, key_grad, value_grad], 2)  37.9 us
    unnamed x299, local copies, waits for them, and re-layouts  34.3 us
    psum x1, blocking collectives, per_device(): lax.psum((qkv_acc, proj_acc, fc1_acc, fc2_acc, qkv_bias_acc, fc1_bias_acc...  28.5 us
  transfers between devices with their start and end apart: 19, of which 7 were waited for; matrix products, arithmetic and copies ran while one was open for 18% of the time, Pallas kernels for 0%

commit v1 on v0

v1 whole, which is shorter than its diff:
```python
import jax
import jax.numpy as jnp
import numpy as np
from jax import lax
from jax.experimental import pallas as pl
from jax.experimental.pallas import tpu as pltpu
from jax.sharding import PartitionSpec as P

D = 512
HEADS = 16
FF = 2048
HEAD_DIM = 32
WINDOW = 7
CELLS = 49
SIDE = 14
SHIFT = 3
SPAN = 13
TABLE = 169
PAD = 64
HALF_ROWS = 7
KEPT = 56
B = 256
SCALE = HEAD_DIM ** (-0.5)
EPS = 1e-05
BLOCKED = -1000000000.0
BF = jnp.bfloat16
F32 = jnp.float32


def nn(a, b):
    return lax.dot_general(a, b, (((1,), (0,)), ((), ())), preferred_element_type=F32)


def nt(a, b):
    return lax.dot_general(a, b, (((1,), (1,)), ((), ())), preferred_element_type=F32)


def tn(a, b):
    return lax.dot_general(a, b, (((0,), (0,)), ((), ())), preferred_element_type=F32)


def norm_parts(values):
    mean = jnp.mean(values, -1, keepdims=True)
    centred = values - mean
    inv = lax.rsqrt(jnp.mean(centred * centred, -1, keepdims=True) + EPS)
    return centred * inv, inv


def norm_back(grad, values, gain):
    x, inv = norm_parts(values)
    s = grad * gain
    back = (s - jnp.mean(s, -1, keepdims=True) - x * jnp.mean(s * x, -1, keepdims=True)) * inv
    return back, x


def head_mask(dtype):
    lane = lax.broadcasted_iota(jnp.int32, (4 * PAD, 128), 1) // HEAD_DIM
    row = lax.broadcasted_iota(jnp.int32, (4 * PAD, 128), 0) // PAD
    return (lane == row).astype(F32).astype(dtype)


def four(x):
    return jnp.concatenate([x, x, x, x], axis=0)


def fold(x, mask):
    y = x * mask
    return y[:PAD] + y[PAD : 2 * PAD] + y[2 * PAD : 3 * PAD] + y[3 * PAD :]


def cut(j):
    return slice(j * B, (j + 1) * B)


def attn_fwd(win, h, allow, rel, w, qb, pb, gains, offs, normed, qkv, probs, mixed, middle):
    hv = h[...].astype(F32)
    x, _ = norm_parts(hv)
    nv = (x * gains[0:1] + offs[0:1]).astype(BF)
    normed[...] = nv
    for c in range(2):
        for t in range(3):
            acc = nn(nv[:, cut(0)], w[0, c, t]) + nn(nv[:, cut(1)], w[1, c, t])
            qkv[c, :, cut(t)] = (acc + qb[c : c + 1, cut(t)]).astype(BF)
    mask_low = head_mask(BF)
    mask = head_mask(F32)
    for c in range(2):
        for g in range(2):
            grp = 2 * c + g
            for n in range(win):
                rows = slice(n * PAD, (n + 1) * PAD)
                q = qkv[c, rows, g * 128 : g * 128 + 128]
                k = qkv[c, rows, B + g * 128 : B + g * 128 + 128]
                v = qkv[c, rows, 2 * B + g * 128 : 2 * B + g * 128 + 128]
                s = nt(four(q) * mask_low, k) * SCALE + rel[grp]
                s = jnp.where(allow[n] > 0.5, s, BLOCKED)
                e = jnp.exp(s - jnp.max(s, -1, keepdims=True))
                p = e / jnp.sum(e, -1, keepdims=True)
                probs[n * 4 + grp] = p
                o = fold(nn(p.astype(BF), v), mask)
                mixed[rows, grp * 128 : grp * 128 + 128] = o.astype(BF)
    mv = mixed[...]
    for r in range(2):
        acc = nn(mv[:, cut(0)], w[r, 0, 3]) + nn(mv[:, cut(1)], w[r, 1, 3])
        middle[:, cut(r)] = hv[:, cut(r)] + (acc + pb[:, cut(r)])


def mlp_fwd(middle, w, b1, b2, gains, offs, n2, act, dact, out):
    mv = middle[...]
    x, _ = norm_parts(mv)
    nv = (x * gains[1:2] + offs[1:2]).astype(BF)
    n2[...] = nv
    acc = [mv[:, cut(r)] + b2[:, cut(r)] for r in range(2)]
    for c in range(2):
        for j in range(4):
            cols = slice(c * 1024 + j * B, c * 1024 + (j + 1) * B)
            pre = nn(nv[:, cut(0)], w[0, c, j]) + nn(nv[:, cut(1)], w[1, c, j]) + b1[:, cols]
            phi = 0.5 + 0.5 * lax.erf(pre * (0.5 ** 0.5))
            av = (pre * phi).astype(BF)
            act[:, cols] = av
            dact[:, cols] = phi + pre * (jnp.exp(-0.5 * pre * pre) * 0.3989422804014327)
            for r in range(2):
                acc[r] = acc[r] + nn(av, w[r, c, 4 + j])
    for r in range(2):
        out[:, cut(r)] = acc[r].astype(BF)


def mlp_bwd(full, g_out, act, dact, n2, middle, w, gains, *outs):
    gz = g_out[...]
    gn = [None, None]
    for c in range(2):
        for j in range(4):
            cols = slice(c * 1024 + j * B, c * 1024 + (j + 1) * B)
            ga = nt(gz[:, cut(0)], w[0, c, 4 + j]) + nt(gz[:, cut(1)], w[1, c, 4 + j])
            gp = (ga * dact[:, cols]).astype(BF)
            for r in range(2):
                t = nt(gp, w[r, c, j])
                gn[r] = t if gn[r] is None else gn[r] + t
            if full:
                av = act[:, cols]
                outs[2][:, cols] = jnp.sum(gp.astype(F32), 0, keepdims=True)
                for r in range(2):
                    outs[1][r, c, 4 + j] = tn(av, gz[:, cut(r)]).astype(BF)
                    outs[1][r, c, j] = tn(n2[:, cut(r)], gp).astype(BF)
    gnv = jnp.concatenate(gn, axis=1)
    back, x = norm_back(gnv, middle[...], gains[1:2])
    gf = gz.astype(F32)
    outs[0][...] = gf + back
    if full:
        outs[3][0:1] = jnp.sum(gnv * x, 0, keepdims=True)
        outs[3][1:2] = jnp.sum(gnv, 0, keepdims=True)
        outs[3][2:3] = jnp.sum(gf, 0, keepdims=True)


def attn_bwd(full, win, gm, mixed, qkv, probs, normed, h, w, gains, *rest):
    outs, (gmix, gqkv) = rest[:-2], rest[-2:]
    gmv = gm[...]
    ga = gmv.astype(BF)
    for c in range(2):
        acc = nt(ga[:, cut(0)], w[0, c, 3]) + nt(ga[:, cut(1)], w[1, c, 3])
        gmix[:, cut(c)] = acc.astype(BF)
    mask_low = head_mask(BF)
    mask = head_mask(F32)
    for c in range(2):
        for g in range(2):
            grp = 2 * c + g
            total = None
            for n in range(win):
                rows = slice(n * PAD, (n + 1) * PAD)
                q = qkv[c, rows, g * 128 : g * 128 + 128]
                k = qkv[c, rows, B + g * 128 : B + g * 128 + 128]
                v = qkv[c, rows, 2 * B + g * 128 : 2 * B + g * 128 + 128]
                g4 = four(gmix[rows, grp * 128 : grp * 128 + 128]) * mask_low
                p = probs[n * 4 + grp]
                gp = nt(g4, v)
                ds = (p * (gp - jnp.sum(p * gp, -1, keepdims=True))).astype(BF)
                gv = tn(p.astype(BF), g4)
                gq = fold(nn(ds, k), mask) * SCALE
                gk = tn(ds, four(q) * mask_low) * SCALE
                gqkv[c, rows, g * 128 : g * 128 + 128] = gq.astype(BF)
                gqkv[c, rows, B + g * 128 : B + g * 128 + 128] = gk.astype(BF)
                gqkv[c, rows, 2 * B + g * 128 : 2 * B + g * 128 + 128] = gv.astype(BF)
                if full:
                    total = ds.astype(F32) if total is None else total + ds.astype(F32)
            if full:
                outs[4][grp] = total
    gn = [None, None]
    for c in range(2):
        for t in range(3):
            gt = gqkv[c, :, cut(t)]
            for r in range(2):
                part = nt(gt, w[r, c, t])
                gn[r] = part if gn[r] is None else gn[r] + part
                if full:
                    outs[1][r, c, t] = tn(normed[:, cut(r)], gt).astype(BF)
            if full:
                outs[2][c : c + 1, cut(t)] = jnp.sum(gt.astype(F32), 0, keepdims=True)
    gnv = jnp.concatenate(gn, axis=1)
    back, x = norm_back(gnv, h[...].astype(F32), gains[0:1])
    outs[0][...] = (gmv + back).astype(BF)
    if full:
        for c in range(2):
            for r in range(2):
                outs[1][r, c, 3] = tn(mixed[:, cut(c)], ga[:, cut(r)]).astype(BF)
        outs[3][0:1] = jnp.sum(gnv * x, 0, keepdims=True)
        outs[3][1:2] = jnp.sum(gnv, 0, keepdims=True)
        outs[3][2:3] = jnp.sum(ga.astype(F32), 0, keepdims=True)


def run(body, args, outs, name, flops, scratch=()):
    shapes = [jax.ShapeDtypeStruct(s, d) for s, d in outs]
    moved = sum(a.size * a.dtype.itemsize for a in list(args) + shapes)
    vm = pl.BlockSpec(memory_space=pltpu.VMEM)
    return pl.pallas_call(
        body,
        out_shape=shapes,
        in_specs=[vm] * len(args),
        out_specs=[vm] * len(outs),
        scratch_shapes=list(scratch),
        compiler_params=pltpu.CompilerParams(vmem_limit_bytes=48 * 1024 * 1024),
        cost_estimate=pl.CostEstimate(flops=flops, bytes_accessed=moved, transcendentals=0),
        name=name,
    )(*args)


def place_matrix(images, shift):
    out = np.zeros((images * 2 * PAD, images * 98), np.float32)
    for n in range(images):
        for r in range(HALF_ROWS):
            for c in range(SIDE):
                rolled = (c - shift) % SIDE
                row = (n * 2 + rolled // WINDOW) * PAD + r * WINDOW + rolled % WINDOW
                out[row, n * 98 + r * SIDE + c] = 1.0
    return out


def allowed_cells(extents, section, col):
    images = extents.shape[0]
    places = jnp.arange(SIDE, dtype=jnp.int32)
    source = (places + SHIFT * section) % SIDE
    padded = (source[None, :, None] >= extents[:, 0, None, None]) | (
        source[None, None, :] >= extents[:, 1, None, None]
    )
    band = (places >= SIDE - WINDOW).astype(jnp.int32) + (places >= SIDE - SHIFT).astype(jnp.int32)
    codes = (band[:, None] * 3 + band[None, :]) * section * 2 + padded.astype(jnp.int32)
    mine = lax.dynamic_slice_in_dim(codes, col * HALF_ROWS, HALF_ROWS, 1)
    mine = mine.reshape(images, HALF_ROWS, 2, WINDOW).transpose(0, 2, 1, 3)
    mine = mine.reshape(images * 2, CELLS)
    query = jnp.pad(mine, ((0, 0), (0, PAD - CELLS)))
    key = jnp.pad(mine, ((0, 0), (0, PAD - CELLS)), constant_values=-1)
    real = jnp.arange(PAD) < CELLS
    same = (query[:, :, None] == key[:, None, :]) | ((~real)[None, :, None] & real[None, None, :])
    return jnp.tile(same.astype(F32), (1, 4, 1))


def relative_onehot():
    cells = np.arange(CELLS)
    a, b = cells // WINDOW, cells % WINDOW
    index = (a[:, None] - a[None, :] + WINDOW - 1) * SPAN + b[:, None] - b[None, :] + WINDOW - 1
    full = np.full((PAD, PAD), -1, np.int32)
    full[:CELLS, :CELLS] = index
    return jnp.asarray(full.reshape(-1))[None, :] == jnp.arange(TABLE, dtype=jnp.int32)[:, None]


def per_device(
    images,
    extents,
    cotangent,
    qkv_weight,
    qkv_bias,
    proj_weight,
    proj_bias,
    fc1_weight,
    fc1_bias,
    fc2_weight,
    fc2_bias,
    norm_gain,
    norm_bias,
    bias_table,
):
    section = lax.axis_index("pipe")
    row = lax.axis_index("row")
    col = lax.axis_index("col")
    first = section == 0
    count = images.shape[0]
    win = count * 2
    rows = win * PAD

    def swap(x, axis):
        return lax.ppermute(x, axis, [(0, 1), (1, 0)])

    attn_w = jnp.concatenate(
        [qkv_weight[0].transpose(1, 0, 2), proj_weight], axis=0
    )
    mlp_w = jnp.concatenate(
        [fc1_weight[0].reshape(B, 4, B).transpose(1, 0, 2), fc2_weight[0].reshape(4, B, B)], axis=0
    )

    def gather_weights(x):
        x = lax.all_gather(x, "col", axis=0)
        return lax.all_gather(x, "row", axis=0)

    attn_w = gather_weights(attn_w)
    mlp_w = gather_weights(mlp_w)
    zeros = jnp.zeros_like(qkv_bias[0, 0])
    packed = jnp.concatenate(
        [qkv_bias[0, 0], zeros, qkv_bias[0, 1], fc1_bias[0], bias_table[0].T.reshape(-1)]
    )
    packed = lax.all_gather(packed, "col", axis=0)
    qb = packed[:, :768]
    b1 = packed[:, 768:1792].reshape(1, FF)
    table = packed[:, 1792:].reshape(HEADS, TABLE)
    pb, b2, gains, offs = proj_bias, fc2_bias, norm_gain[0], norm_bias[0]
    onehot = relative_onehot().astype(F32)
    rel = jnp.dot(table, onehot, precision=lax.Precision.HIGHEST).reshape(4, 4 * PAD, PAD)
    allow = allowed_cells(extents, section, col)
    place = jnp.where(
        first, jnp.asarray(place_matrix(count, 0), BF), jnp.asarray(place_matrix(count, SHIFT), BF)
    )

    def to_win(nat):
        return nn(place, nat.reshape(count * 98, D)).astype(BF)

    def from_win(x):
        return tn(place, x).astype(BF).reshape(count, 98, D)

    def forward(h):
        normed, qkv, probs, mixed, middle = run(
            lambda *a: attn_fwd(win, *a),
            (h, allow, rel, attn_w, qb, pb, gains, offs),
            [
                ((rows, D), BF),
                ((2, rows, 768), BF),
                ((win * 4, 4 * PAD, PAD), F32),
                ((rows, D), BF),
                ((rows, D), F32),
            ],
            "attn_fwd",
            2 * rows * D * D * 4,
        )
        n2, act, dact, out = run(
            mlp_fwd,
            (middle, mlp_w, b1, b2, gains, offs),
            [((rows, D), BF), ((rows, FF), BF), ((rows, FF), F32), ((rows, D), BF)],
            "mlp_fwd",
            2 * rows * D * FF * 2,
        )
        return (h, normed, qkv, probs, mixed, middle, n2, act, dact), from_win(out)

    def backward(kept, g_out, full):
        h, normed, qkv, probs, mixed, middle, n2, act, dact = kept
        extra = [((2, 2, 8, B, B), BF), ((1, FF), F32), ((3, D), F32)] if full else []
        res = run(
            lambda *a: mlp_bwd(full, *a),
            (g_out, act, dact, n2, middle, mlp_w, gains),
            [((rows, D), F32)] + extra,
            "mlp_bwd",
            2 * rows * D * FF * (4 if full else 2),
        )
        extra = (
            [((2, 2, 4, B, B), BF), ((2, 768), F32), ((3, D), F32), ((4, 4 * PAD, PAD), F32)]
            if full
            else []
        )
        res2 = run(
            lambda *a: attn_bwd(full, win, *a),
            (res[0], mixed, qkv, probs, normed, h, attn_w, gains),
            [((rows, D), BF)] + extra,
            "attn_bwd",
            2 * rows * D * D * 8,
            [pltpu.VMEM((rows, D), BF), pltpu.VMEM((2, rows, 768), BF)],
        )
        return res[1:], res2[1:], from_win(res2[0])

    both = ("pipe", "col")
    _, nat = forward(to_win(images))
    kept_part = lax.ppermute(nat[:, 98 - KEPT :], both, [(0, 2), (1, 3)])
    sent_part = lax.ppermute(nat[:, : 98 - KEPT], both, [(0, 3), (1, 2)])
    received = jnp.concatenate([kept_part, sent_part], axis=1)
    kept, nat_out = forward(to_win(jnp.where(first, images, received)))

    cot_swap = swap(cotangent[:, : 98 - KEPT], "col")
    cot = jnp.concatenate([cotangent[:, 98 - KEPT :], cot_swap], axis=1)
    _, _, g_nat = backward(kept, to_win(cot), False)
    g_kept = lax.ppermute(g_nat[:, :KEPT], both, [(2, 0), (3, 1)])
    g_sent = lax.ppermute(g_nat[:, KEPT:], both, [(2, 1), (3, 0)])
    g_received = jnp.concatenate([g_sent, g_kept], axis=1)
    mlp_res, attn_res, g_in = backward(kept, to_win(jnp.where(first, g_received, cot)), True)

    def unroll(x):
        back = swap(x[:, KEPT:], "col")
        return jnp.where(first, x, jnp.concatenate([back, x[:, :KEPT]], axis=1))

    layer_outputs = unroll(nat_out)[None]
    input_grads = unroll(g_in)[None]

    def reduce_grads(x):
        mine = lax.dynamic_index_in_dim(x, row, 0, keepdims=False)
        other = lax.dynamic_index_in_dim(x, 1 - row, 0, keepdims=False)
        y = mine.astype(F32) + swap(other, "row").astype(F32)
        mine = lax.dynamic_index_in_dim(y, col, 0, keepdims=False)
        other = lax.dynamic_index_in_dim(y, 1 - col, 0, keepdims=False).astype(BF)
        z = mine + swap(other, "col").astype(F32)
        return lax.psum(z.astype(BF), "dp").astype(F32)

    g_mlp = reduce_grads(mlp_res[0])
    g_attn = reduce_grads(attn_res[0])
    table_part = lax.dot_general(
        attn_res[3].reshape(HEADS, PAD * PAD),
        onehot,
        (((1,), (1,)), ((), ())),
        precision=lax.Precision.HIGHEST,
    )
    smalls = (mlp_res[1], mlp_res[2], attn_res[1], attn_res[2], table_part)
    flat = jnp.concatenate([s.reshape(-1) for s in smalls])
    flat = lax.psum(flat, ("dp", "row", "col"))
    parts, at = [], 0
    for s in smalls:
        parts.append(flat[at : at + s.size].reshape(s.shape))
        at += s.size
    b1_grad, mlp_small, qkv_small, attn_small, table_sum = parts
    pick = lambda x: lax.dynamic_index_in_dim(x, col, 0, keepdims=False)
    b1_grad = pick(b1_grad.reshape(2, 1024))
    qkv_small = pick(qkv_small).reshape(3, B)
    qkv_bias_grad = jnp.stack([qkv_small[0], qkv_small[2]], 0)
    table_grad = pick(table_sum.reshape(2, HEADS // 2, TABLE)).T
    gain_grad = jnp.stack([attn_small[0], mlp_small[0]], 0)
    offset_grad = jnp.stack([attn_small[1], mlp_small[1]], 0)
    return (
        layer_outputs,
        input_grads,
        g_attn[:3].transpose(1, 0, 2)[None],
        qkv_bias_grad[None],
        g_attn[3][None],
        attn_small[2][None],
        g_mlp[:4].transpose(1, 0, 2).reshape(B, 1024)[None],
        b1_grad[None],
        g_mlp[4:].reshape(1024, B)[None],
        mlp_small[2][None],
        gain_grad[None],
        offset_grad[None],
        table_grad[None],
    )


def solution(mesh):
    placed = (
        P(("dp", "row"), "col", None),
        P(("dp", "row"), None),
        P(("dp", "row"), "col", None),
        P("pipe", "row", None, "col"),
        P("pipe", None, "col"),
        P("pipe", "col", "row"),
        P("pipe", None),
        P("pipe", "row", "col"),
        P("pipe", "col"),
        P("pipe", "col", "row"),
        P("pipe", None),
        P("pipe", None, None),
        P("pipe", None, None),
        P("pipe", None, "col"),
    )
    return jax.shard_map(
        per_device,
        mesh=mesh,
        in_specs=placed,
        out_specs=(
            P("pipe", ("dp", "row"), "col", None),
            P("pipe", ("dp", "row"), "col", None),
            P("pipe", "row", None, "col"),
            P("pipe", None, "col"),
            P("pipe", "col", "row"),
            P("pipe", None),
            P("pipe", "row", "col"),
            P("pipe", "col"),
            P("pipe", "col", "row"),
            P("pipe", None),
            P("pipe", None, None),
            P("pipe", None, None),
            P("pipe", None, "col"),
        ),
        check_vma=False,
    )
```

time: 757 us -> 317 us (0.42); the launches traced: 744 us -> 316 us
  blocking collectives: 266 us -> 72.1 us
  matrix products: 133 us -> 6.56 us
  local copies, waits for them, and re-layouts: 139 us -> 35.7 us
  other arithmetic: 90.2 us -> 19.5 us
  waiting for transfers between devices: 37.5 us -> 105 us
  Pallas kernels: 0 us -> 48.9 us
  starting transfers between devices: 61.4 us -> 13 us
    dot_general x64 -> x10, matrix products: 121 us -> 6.56 us  [the longest x4 2.54 us: nn(): lax.dot_general(a, b, (((1,), (0,)), ((), ())), preferred_element_type=F32)]
    all_gather x14 -> x0, blocking collectives: 90.4 us -> none  [the longest x6 43.3 us: gather_grads(): return lax.all_gather(values, 'col', axis=1, tiled=True)]
    unnamed x11 -> x1, blocking collectives: 87.2 us -> 8.64 us
    all_gather x2 -> x4, waiting for transfers between devices: 0.01 us -> 66.1 us  [the longest x2 57.1 us: gather_weights(): x = lax.all_gather(x, 'col', axis=0)]
    pallas_call x0 -> x8, Pallas kernels: none -> 48.9 us  [run(): pl.pallas_call(body, out_shape=shapes, in_specs=[vm] * len(args), out_spe...]
    unnamed x12 -> x0, starting transfers between devices: 38.9 us -> none
    another operation x29 -> x4, local copies, waits for them, and re-layouts: 38 us -> 1.4 us  [the longest x1 1.25 us: per_device(): fc2_weight[0].reshape(4, B, B)]
    ppermute x4 -> x11, waiting for transfers between devices: 8.02 us -> 38.6 us  [the longest x7 29.8 us: swap(): return lax.ppermute(x, axis, [(0, 1), (1, 0)])]
  transfers between devices with their start and end apart: 19 -> 16, of which waited for: 7 -> 9; matrix products, arithmetic and copies ran while one was open for 18% -> 10% of each run, Pallas kernels for 0% -> 4%
where the time goes in v1:
time: 317 us; the launch traced here: 316 us
  waiting for transfers between devices  105 us (33%)
  blocking collectives  72.1 us (23%)
  Pallas kernels  48.9 us (15%)
  local copies, waits for them, and re-layouts  35.7 us (11%)
  other arithmetic  19.5 us (6%)
  between operations  15.5 us (5%)
  starting transfers between devices  13 us (4%)
  matrix products  6.56 us (2%)
    psum x1, blocking collectives, per_device(): flat = lax.psum(flat, ('dp', 'row', 'col'))  63.4 us
    all_gather x2, waiting for transfers between devices, gather_weights(): x = lax.all_gather(x, 'col', axis=0)  57.1 us
    pallas_call x8, Pallas kernels, run(): pl.pallas_call(body, out_shape=shapes, in_specs=[vm] * len(args), out_spe...  48.9 us
    ppermute x7, waiting for transfers between devices, swap(): return lax.ppermute(x, axis, [(0, 1), (1, 0)])  29.8 us
    unnamed x124, local copies, waits for them, and re-layouts  9.82 us
    all_gather x2, waiting for transfers between devices, gather_weights(): return lax.all_gather(x, 'row', axis=0)  9 us
    unnamed x1, blocking collectives  8.64 us
    convert_element_type x4, other arithmetic, reduce_grads(): return lax.psum(z.astype(BF), 'dp').astype(F32)  6.43 us
  transfers between devices with their start and end apart: 16, of which 9 were waited for; matrix products, arithmetic and copies ran while one was open for 10% of the time, Pallas kernels for 4%

profile of v1, /device:TPU:0, one launch (start us, length us, event | category | flops | bytes accessed | tf_op | source)
XLA Modules:
  0.0 316.3 jit_solution(4546851577194124017)
XLA Ops:
  7.2 1.9 pad_maximum_fusion.1
  10.8 1.3 copy.74
  12.2 22.0 %all-gather.10.cloned.1.call-done = bf16[8,256,256]{2,1,0:T(8,128)(2,1)} async-done(((bf16[4,256,256]{2,1,0:T(8,128)(2,1)}), bf16[8,256,256]{2,1,0:T(8,128)(2,1)}) %all-gather.10.cloned.1.call-update) | async-done | bytes 1048592 | tf_op jit(solution)/shard_map/all_gather | solution.py:299
  34.3 35.2 %all-gather.14.cloned.1.call-done = bf16[16,256,256]{2,1,0:T(8,128)(2,1)} async-done(((bf16[8,256,256]{2,1,0:T(8,128)(2,1)}), bf16[16,256,256]{2,1,0:T(8,128)(2,1)}) %all-gather.14.cloned.1.call-update) | async-done | bytes 2097168 | tf_op jit(solution)/shard_map/all_gather | solution.py:299
  72.7 8.6 %all-reduce.2 = f32[6288]{0:T(1024)S(1)} all-reduce(f32[6288]{0:T(1024)S(1)} %dynamic-update-slice), channel_id=2, replica_groups=mesh['pipe'=2,'dp'=4,'row'=2,'col'=2] {'col'}, use_global_device_ids=true, to_apply=%add.2 | all-reduce | flops 6288 | bytes 50304
  83.8 5.1 %attn_fwd.2 = (bf16[256,512]{1,0:T(8,128)(2,1)}, bf16[2,256,768]{2,1,0:T(8,128)(2,1)}, f32[16,256,64]{2,1,0:T(8,128)}, bf16[256,512]{1,0:T(8,128)(2,1)}, f32[256,512]{1,0:T(8,128)S(1)}) custom-call(bf16[256,512]{1,0:T(8,128)(2,1)S(1)} %convolution_convert_fusion.3.a_0_, f32[4,256,64]{2,1,0:T(8,128)S(1)} %bitcast.92, f32[4,256,64]{2,1,0:T(8,128)S(1)} %reshape.373.a_2_, ...), custom_call_target="tpu_custom_call" | custom-call | flops 536870912 | bytes 5783552 | tf_op jit(solution)/shard_map/attn_fwd/pallas_call | solution.py:213
  88.9 9.0 %all-gather.16.cloned.1.call-done = bf16[4,8,256,256]{3,2,1,0:T(8,128)(2,1)} async-done(((bf16[2,8,256,256]{3,2,1,0:T(8,128)(2,1)}), bf16[4,8,256,256]{3,2,1,0:T(8,128)(2,1)}) %all-gather.16.cloned.1.call-update) | async-done | bytes 4194320 | tf_op jit(solution)/shard_map/all_gather | solution.py:300
  97.9 5.4 %mlp_fwd.2 = (bf16[256,512]{1,0:T(8,128)(2,1)}, bf16[256,2048]{1,0:T(8,128)(2,1)}, f32[256,2048]{1,0:T(8,128)}, bf16[256,512]{1,0:T(8,128)(2,1)S(1)}) custom-call(f32[256,512]{1,0:T(8,128)S(1)} %get-tuple-element.33.middle, bf16[2,2,8,256,256]{4,3,2,1,0:T(8,128)(2,1)} %bitcast.109, f32[1,2048]{1,0:T(1,128)S(1)} %bitcast.102, f32[1,512]{1,0:T(1,128)S(1)} %copy-done.26, ...), custom_call_target="tpu_custom_call" | custom-call | flops 1073741824 | bytes 8407040 | tf_op jit(solution)/shard_map/mlp_fwd/pallas_call | solution.py:213
  103.7 4.5 %collective-permute-start.1 = (bf16[2,42,512]{2,1,0:T(8,128)(2,1)S(1)}, bf16[2,42,512]{2,1,0:T(8,128)(2,1)S(1)}, u32[]{:S(2)}, u32[]{:S(2)}) collective-permute-start(bf16[2,42,512]{2,1,0:T(8,128)(2,1)S(1)} %slice.169), channel_id=1, source_target_pairs={{0,17},{1,16},{2,19},{3,18},{4,21},{5,20},{6,23},{7,22},{8,25},{9,... | collective-permute-start | bytes 258056 | tf_op jit(solution)/shard_map/ppermute | solution.py:377
  108.2 1.5 collective-permute-start
  111.3 1.8 collective-permute-done
  113.5 4.1 %attn_fwd.3 = (bf16[256,512]{1,0:T(8,128)(2,1)S(1)}, bf16[2,256,768]{2,1,0:T(8,128)(2,1)S(1)}, f32[16,256,64]{2,1,0:T(8,128)S(1)}, bf16[256,512]{1,0:T(8,128)(2,1)S(1)}, f32[256,512]{1,0:T(8,128)S(1)}) custom-call(bf16[256,512]{1,0:T(8,128)(2,1)S(1)} %convolution_convert_fusion.2.a_0_.a_5_, f32[4,256,64]{2,1,0:T(8,128)S(1)} %bitcast.93, ...), custom_call_target="tpu_custom_call" | custom-call | flops 536870912 | bytes 5783552 | tf_op jit(solution)/shard_map/attn_fwd/pallas_call | solution.py:213
  117.6 5.3 %mlp_fwd.3 = (bf16[256,512]{1,0:T(8,128)(2,1)S(1)}, bf16[256,2048]{1,0:T(8,128)(2,1)S(1)}, f32[256,2048]{1,0:T(8,128)S(1)}, bf16[256,512]{1,0:T(8,128)(2,1)S(1)}) custom-call(f32[256,512]{1,0:T(8,128)S(1)} %get-tuple-element.35.middle.a_4_, bf16[2,2,8,256,256]{4,3,2,1,0:T(8,128)(2,1)} %bitcast.110, f32[1,2048]{1,0:T(1,128)S(1)} %bitcast.103, ...), custom_call_target="tpu_custom_call" | custom-call | flops 1073741824 | bytes 8407040 | tf_op jit(solution)/shard_map/mlp_fwd/pallas_call | solution.py:213
  123.6 5.8 %mlp_bwd.2.a_0_ = f32[256,512]{1,0:T(8,128)S(1)} custom-call(bf16[256,512]{1,0:T(8,128)(2,1)S(1)} %copy-done.9, bf16[256,2048]{1,0:T(8,128)(2,1)S(1)} %get-tuple-element.37.a_1_, f32[256,2048]{1,0:T(8,128)S(1)} %get-tuple-element.38.a_2_, bf16[256,512]{1,0:T(8,128)(2,1)S(1)} %get-tuple-element.39.a_3_, f32[256,512]{1,0:T(8,128)S(1)} %get-tuple-element.35.middle.a_4_, ...), custom_call_target="tpu_custom_call" | custom-call | flops 1073741824 | bytes 8916992 | tf_op jit(solution)/shard_map/mlp_bwd/pallas_call | solution.py:213
  129.5 7.3 %attn_bwd.2 = bf16[256,512]{1,0:T(8,128)(2,1)S(1)} custom-call(f32[256,512]{1,0:T(8,128)S(1)} %mlp_bwd.2.a_0_, bf16[256,512]{1,0:T(8,128)(2,1)S(1)} %get-tuple-element.40.a_1_, bf16[2,256,768]{2,1,0:T(8,128)(2,1)S(1)} %get-tuple-element.41.a_2_, f32[16,256,64]{2,1,0:T(8,128)S(1)} %get-tuple-element.42.a_3_, bf16[256,512]{1,0:T(8,128)(2,1)S(1)} %get-tuple-element.43.a_4_, ...), custom_call_target="tpu_custom_call" | custom-call | flops 1073741824 | bytes 5509120 | tf_op jit(solution)/shard_map/attn_bwd/pallas_call | solution.py:213
  137.7 1.7 reshape.380
  141.6 1.5 slice.172
  143.1 1.5 collective-permute-start.4
  144.6 6.2 %collective-permute-done.4 = bf16[2,42,512]{2,1,0:T(8,128)(2,1)} collective-permute-done((bf16[2,42,512]{2,1,0:T(8,128)(2,1)}, bf16[2,42,512]{2,1,0:T(8,128)(2,1)}, u32[]{:S(2)}, u32[]{:S(2)}) %collective-permute-start.4) | collective-permute-done | bytes 86048 | tf_op jit(solution)/shard_map/ppermute | solution.py:385
  150.8 1.7 pad_maximum_fusion.2
  152.5 1.7 concatenate.60
  156.6 7.6 %mlp_bwd.3 = (f32[256,512]{1,0:T(8,128)S(1)}, bf16[2,2,8,256,256]{4,3,2,1,0:T(8,128)(2,1)}, f32[1,2048]{1,0:T(1,128)S(1)}, f32[3,512]{1,0:T(4,128)S(1)}) custom-call(bf16[256,512]{1,0:T(8,128)(2,1)S(1)} %convolution_convert_fusion.a_0_, bf16[256,2048]{1,0:T(8,128)(2,1)S(1)} %copy-done.6, f32[256,2048]{1,0:T(8,128)S(1)} %copy-done.2, ...), custom_call_target="tpu_custom_call" | custom-call | flops 2147483648 | bytes 13125632 | tf_op jit(solution)/shard_map/mlp_bwd/pallas_call | solution.py:213
  164.2 3.4 %dynamic-slice_bitcast_fusion = bf16[2,8,256,256]{3,2,1,0:T(8,128)(2,1)} fusion(bf16[2,2,8,256,256]{4,3,2,1,0:T(8,128)(2,1)} %get-tuple-element.52, s32[]{:T(128)S(6)} %select_n.103), kind=kLoop, calls=%fused_computation.8 | loop fusion | bytes 4194308 | tf_op jit(solution)/shard_map/jit(dynamic_index_in_dim)/squeeze | solution.py:398
  171.2 8.4 %attn_bwd.3 = (bf16[256,512]{1,0:T(8,128)(2,1)S(1)}, bf16[2,2,4,256,256]{4,3,2,1,0:T(8,128)(2,1)S(1)}, f32[2,768]{1,0:T(2,128)S(1)}, f32[3,512]{1,0:T(4,128)S(1)}, f32[4,256,64]{2,1,0:T(8,128)S(1)}) custom-call(f32[256,512]{1,0:T(8,128)S(1)} %copy-done.19, bf16[256,512]{1,0:T(8,128)(2,1)S(1)} %copy-done.13, bf16[2,256,768]{2,1,0:T(8,128)(2,1)S(1)} %copy-done.8, ...), custom_call_target="tpu_custom_call" | custom-call | flops 1073741824 | bytes 7880704 | tf_op jit(solution)/shard_map/attn_bwd/pallas_call | solution.py:213
  187.8 2.8 convert_add_fusion
  192.7 2.8 convert_add_fusion.1
  198.0 1.4 fusion
  199.6 29.0 %collective-permute-done.8 = bf16[4,256,256]{2,1,0:T(8,128)(2,1)S(1)} collective-permute-done((bf16[4,256,256]{2,1,0:T(8,128)(2,1)S(1)}, bf16[4,256,256]{2,1,0:T(8,128)(2,1)S(1)}, u32[]{:S(2)}, u32[]{:S(2)}) %collective-permute-start.8) | collective-permute-done | bytes 524320 | tf_op jit(solution)/shard_map/ppermute | solution.py:289
  228.6 2.2 fusion.6
  230.8 2.9 fusion.2
  233.7 63.4 %psum.22 = f32[9360]{0:T(1024)S(1)} all-reduce(f32[9360]{0:T(1024)S(1)} %constant_dynamic-update-slice_fusion.5), channel_id=1, replica_groups=mesh['pipe'=2,'dp'=4,'row'=2,'col'=2] {'dp','row','col'}, use_global_device_ids=true, to_apply=%region_1.2 | all-reduce | flops 9360 | bytes 74880 | tf_op jit(solution)/shard_map/psum | solution.py:415
  304.2 1.6 slice.178
  (240 shorter events, 42.3 us)
Async XLA Ops:
  7.2 27.0 %all-gather.10.cloned.1.call-start = ((), (), s32[]{:S(2)}) async-start(), calls=%async_computation | async-start | bytes 1572864 | tf_op jit(solution)/shard_map/all_gather | solution.py:299
  9.2 60.2 %all-gather.14.cloned.1.call-start = ((), (), s32[]{:S(2)}) async-start(), calls=%async_computation.2 | async-start | bytes 3145728 | tf_op jit(solution)/shard_map/all_gather | solution.py:299
  12.1 57.4 %copy-start.44 = (bf16[2,98,512]{2,0,1:T(2,128)(2,1)S(1)}, bf16[2,98,512]{2,0,1:T(2,128)(2,1)}, u32[]{:S(2)}) copy-start(bf16[2,98,512]{2,0,1:T(2,128)(2,1)} %param.19) | copy-start | bytes 602116
  12.1 57.9 %copy-start.42 = (bf16[2,98,512]{2,0,1:T(2,128)(2,1)S(1)}, bf16[2,98,512]{2,0,1:T(2,128)(2,1)}, u32[]{:S(2)}) copy-start(bf16[2,98,512]{2,0,1:T(2,128)(2,1)} %param.17) | copy-start | bytes 602116
  12.2 58.0 %copy-start.47 = (s32[2,2]{1,0:T(2,128)S(1)}, s32[2,2]{1,0:T(2,128)}, u32[]{:S(2)}) copy-start(s32[2,2]{1,0:T(2,128)} %param.18) | copy-start | bytes 52
  12.2 71.5 %all-gather.12.cloned.1.call-start = ((), (), s32[]{:S(2)}) async-start(), calls=%async_computation.1 | async-start | bytes 3145728 | tf_op jit(solution)/shard_map/all_gather | solution.py:300
  34.2 36.7 %copy-start.46 = (f32[1,169,8]{1,2,0:T(8,128)S(1)}, f32[1,169,8]{1,2,0:T(8,128)}, u32[]{:S(2)}) copy-start(f32[1,169,8]{1,2,0:T(8,128)} %param.30) | copy-start | bytes 16228
  34.2 36.8 %copy-start.52 = (u32[32]{0:T(128)S(1)}, u32[32]{0:T(128)}, u32[]{:S(2)}) copy-start(u32[32]{0:T(128)} %constant.108) | copy-start | bytes 388
  34.2 38.0 %copy-start.49 = (f32[1,2,256]{2,1,0:T(2,128)S(1)}, f32[1,2,256]{2,1,0:T(2,128)}, u32[]{:S(2)}) copy-start(f32[1,2,256]{2,1,0:T(2,128)} %param.21) | copy-start | bytes 6148
  34.2 38.1 %copy-start.48 = (f32[1,1024]{1,0:T(1,128)S(1)}, f32[1,1024]{1,0:T(1,128)}, u32[]{:S(2)}) copy-start(f32[1,1024]{1,0:T(1,128)} %param.25) | copy-start | bytes 12292
  34.2 47.5 %copy-start.50 = (s32[4096]{0:T(1024)S(1)}, s32[4096]{0:T(1024)}, u32[]{:S(2)}) copy-start(s32[4096]{0:T(1024)} %constant.85.clone) | copy-start | bytes 49156
  34.2 63.7 %all-gather.16.cloned.1.call-start = ((), (), s32[]{:S(2)}) async-start(), calls=%async_computation.3 | async-start | bytes 6291456 | tf_op jit(solution)/shard_map/all_gather | solution.py:300
  69.5 13.4 %copy-start.32 = (bf16[256,196]{1,0:T(8,128)(2,1)S(1)}, bf16[256,196]{1,0:T(8,128)(2,1)}, u32[]{:S(2)}) copy-start(bf16[256,196]{1,0:T(8,128)(2,1)} %constant.87.clone) | copy-start | bytes 301060
  69.5 13.8 %slice-start = ((bf16[2,98,512]{2,0,1:T(2,128)(2,1)}), bf16[2,56,512]{2,0,1:T(2,128)(2,1)S(1)}, s32[]{:S(2)}) async-start(bf16[2,98,512]{2,0,1:T(2,128)(2,1)} %param.19), calls=%async_computation.5 | async-start | bytes 229376 | tf_op jit(solution)/shard_map/slice | solution.py:382
  69.5 233.5 %all-reduce.6.cloned.1.call-start = ((), (), s32[]{:S(2)}) async-start(), calls=%async_computation.4 | async-start | bytes 3145728 | tf_op jit(solution)/shard_map/psum | solution.py:403
  69.6 13.7 %collective-permute-start.3 = (bf16[2,42,512]{2,0,1:T(2,128)(2,1)S(1)}, bf16[2,42,512]{2,0,1:T(2,128)(2,1)S(1)}, u32[]{:S(2)}, u32[]{:S(2)}) collective-permute-start(bf16[2,42,512]{2,0,1:T(2,128)(2,1)S(1)} %slice.139), channel_id=1, source_target_pairs={{0,1},{1,0},{2,3},{3,2},{4,5},{5,4},{6,7},{7,6},{8,9},{9,8},{10,11... | collective-permute-start | bytes 258056 | tf_op jit(solution)/shard_map/ppermute | solution.py:289
  83.7 29.8 %copy-start.36 = (bf16[196,512]{1,0:T(8,128)(2,1)}, bf16[196,512]{1,0:T(8,128)(2,1)S(1)}, u32[]{:S(2)}) copy-start(bf16[196,512]{1,0:T(8,128)(2,1)S(1)} %reshape.379) | copy-start | bytes 602116
  83.7 14.2 %copy-start.26 = (f32[1,512]{1,0:T(1,128)S(1)}, f32[1,512]{1,0:T(1,128)}, u32[]{:S(2)}) copy-start(f32[1,512]{1,0:T(1,128)} %b2.3) | copy-start | bytes 6148
  103.7 7.7 %collective-permute-start.1 = (bf16[2,42,512]{2,1,0:T(8,128)(2,1)S(1)}, bf16[2,42,512]{2,1,0:T(8,128)(2,1)S(1)}, u32[]{:S(2)}, u32[]{:S(2)}) collective-permute-start(bf16[2,42,512]{2,1,0:T(8,128)(2,1)S(1)} %slice.169), channel_id=1, source_target_pairs={{0,17},{1,16},{2,19},{3,18},{4,21},{5,20},{6,23},{7,22},{8,25},{9,... | collective-permute-start | bytes 258056 | tf_op jit(solution)/shard_map/ppermute | solution.py:377
  108.2 5.0 %collective-permute-start = (bf16[2,56,512]{2,1,0:T(8,128)(2,1)S(1)}, bf16[2,56,512]{2,1,0:T(8,128)(2,1)S(1)}, u32[]{:S(2)}, u32[]{:S(2)}) collective-permute-start(bf16[2,56,512]{2,1,0:T(8,128)(2,1)S(1)} %slice.168), channel_id=1, source_target_pairs={{0,16},{1,17},{2,18},{3,19},{4,20},{5,21},{6,22},{7,23},{8,24},{9,... | collective-permute-start | bytes 344072 | tf_op jit(solution)/shard_map/ppermute | solution.py:376
  136.8 18.6 %copy-start.2 = (f32[256,2048]{1,0:T(8,128)S(1)}, f32[256,2048]{1,0:T(8,128)}, u32[]{:S(2)}) copy-start(f32[256,2048]{1,0:T(8,128)} %copy-done.1) | copy-start | bytes 6291460
  136.8 18.6 %copy-start.4 = (f32[256,512]{1,0:T(8,128)S(1)}, f32[256,512]{1,0:T(8,128)}, u32[]{:S(2)}) copy-start(f32[256,512]{1,0:T(8,128)} %copy-done.3) | copy-start | bytes 1572868
  136.8 18.6 %copy-start.15 = (bf16[256,512]{1,0:T(8,128)(2,1)S(1)}, bf16[256,512]{1,0:T(8,128)(2,1)}, u32[]{:S(2)}) copy-start(bf16[256,512]{1,0:T(8,128)(2,1)} %copy-done.14) | copy-start | bytes 786436
  140.3 10.6 %collective-permute-start.5 = (bf16[2,56,512]{2,1,0:T(8,128)(2,1)S(1)}, bf16[2,56,512]{2,1,0:T(8,128)(2,1)}, u32[]{:S(2)}, u32[]{:S(2)}) collective-permute-start(bf16[2,56,512]{2,1,0:T(8,128)(2,1)S(1)} %slice.173), channel_id=1, source_target_pairs={{16,0},{17,1},{18,2},{19,3},{20,4},{21,5},{22,6},{23,7},{24,8},{25... | collective-permute-start | bytes 344072 | tf_op jit(solution)/shard_map/ppermute | solution.py:384
  143.1 7.7 %collective-permute-start.4 = (bf16[2,42,512]{2,1,0:T(8,128)(2,1)}, bf16[2,42,512]{2,1,0:T(8,128)(2,1)}, u32[]{:S(2)}, u32[]{:S(2)}) collective-permute-start(bf16[2,42,512]{2,1,0:T(8,128)(2,1)} %slice.172), channel_id=1, source_target_pairs={{16,1},{17,0},{18,3},{19,2},{20,5},{21,4},{22,7},{23,6},{24,9},{25... | collective-permute-start | bytes 258056 | tf_op jit(solution)/shard_map/ppermute | solution.py:385
  167.6 20.2 %collective-permute-start.9 = (bf16[2,8,256,256]{3,2,1,0:T(8,128)(2,1)}, bf16[2,8,256,256]{3,2,1,0:T(8,128)(2,1)}, u32[]{:S(2)}, u32[]{:S(2)}) collective-permute-start(bf16[2,8,256,256]{3,2,1,0:T(8,128)(2,1)} %dynamic-slice_bitcast_fusion), channel_id=1, source_target_pairs={{0,2},{2,0},{1,3},{3,1},{4,6},{6,4},{5,7},{7,5},{8,10},{10,8},{9,1... | collective-permute-start | bytes 6291464 | tf_op jit(solution)/shard_map/ppermute | solution.py:289
  168.0 15.9 %collective-permute-start.2 = (bf16[2,42,512]{2,1,0:T(8,128)(2,1)S(1)}, bf16[2,42,512]{2,1,0:T(8,128)(2,1)}, u32[]{:S(2)}, u32[]{:S(2)}) collective-permute-start(bf16[2,42,512]{2,1,0:T(8,128)(2,1)S(1)} %slice.170), channel_id=1, source_target_pairs={{0,1},{1,0},{2,3},{3,2},{4,5},{5,4},{6,7},{7,6},{8,9},{9,8},{10,11... | collective-permute-start | bytes 258056 | tf_op jit(solution)/shard_map/ppermute | solution.py:289
  182.2 10.4 %collective-permute-start.7 = (bf16[2,4,256,256]{3,2,1,0:T(8,128)(2,1)}, bf16[2,4,256,256]{3,2,1,0:T(8,128)(2,1)}, u32[]{:S(2)}, u32[]{:S(2)}) collective-permute-start(bf16[2,4,256,256]{3,2,1,0:T(8,128)(2,1)} %dynamic-slice_bitcast_fusion.1), channel_id=1, source_target_pairs={{0,2},{2,0},{1,3},{3,1},{4,6},{6,4},{5,7},{7,5},{8,10},{10,8},{9,1... | collective-permute-start | bytes 3145736 | tf_op jit(solution)/shard_map/ppermute | solution.py:289
  191.8 39.0 %collective-permute-start.10 = (bf16[8,256,256]{2,1,0:T(8,128)(2,1)}, bf16[8,256,256]{2,1,0:T(8,128)(2,1)S(1)}, u32[]{:S(2)}, u32[]{:S(2)}) collective-permute-start(bf16[8,256,256]{2,1,0:T(8,128)(2,1)} %fusion.5), channel_id=1, source_target_pairs={{0,1},{1,0},{2,3},{3,2},{4,5},{5,4},{6,7},{7,6},{8,9},{9,8},{10,11... | collective-permute-start | bytes 3145736 | tf_op jit(solution)/shard_map/ppermute | solution.py:289
  196.8 31.8 %collective-permute-start.8 = (bf16[4,256,256]{2,1,0:T(8,128)(2,1)S(1)}, bf16[4,256,256]{2,1,0:T(8,128)(2,1)S(1)}, u32[]{:S(2)}, u32[]{:S(2)}) collective-permute-start(bf16[4,256,256]{2,1,0:T(8,128)(2,1)S(1)} %fusion.7), channel_id=1, source_target_pairs={{0,1},{1,0},{2,3},{3,2},{4,5},{5,4},{6,7},{7,6},{8,9},{9,8},{10,11... | collective-permute-start | bytes 1572872 | tf_op jit(solution)/shard_map/ppermute | solution.py:289
  233.7 68.2 %copy-start.41 = (bf16[1,2,98,512]{3,2,1,0:T(8,128)(2,1)S(1)}, bf16[1,2,98,512]{3,2,1,0:T(8,128)(2,1)}, u32[]{:S(2)}) copy-start(bf16[1,2,98,512]{3,2,1,0:T(8,128)(2,1)} %reshape.381) | copy-start | bytes 602116
  297.2 4.7 %collective-permute-start.6 = (bf16[2,42,512]{2,1,0:T(8,128)(2,1)S(1)}, bf16[2,42,512]{2,1,0:T(8,128)(2,1)S(1)}, u32[]{:S(2)}, u32[]{:S(2)}) collective-permute-start(bf16[2,42,512]{2,1,0:T(8,128)(2,1)S(1)} %slice.174), channel_id=1, source_target_pairs={{0,1},{1,0},{2,3},{3,2},{4,5},{5,4},{6,7},{7,6},{8,9},{9,8},{10,11... | collective-permute-start | bytes 258056 | tf_op jit(solution)/shard_map/ppermute | solution.py:289
  (38 other events, 173.3 us)
Sparse Core Ops, SparseCore 0:
  10.1 23.9 all-gather.9
  36.3 33.1 all-gather.13
  71.0 10.6 all-gather.11
  83.1 14.7 all-gather.15
  233.8 69.1 all-reduce.5

commit v2 on v1

--- a/solution.py
+++ b/solution.py
@@ -206,7 +206,177 @@
         outs[3][2:3] = jnp.sum(ga.astype(F32), 0, keepdims=True)
 
 
-def run(body, args, outs, name, flops, scratch=()):
+def partner_copy(src, dst, send, recv, device):
+    return pltpu.make_async_remote_copy(
+        src_ref=src,
+        dst_ref=dst,
+        send_sem=send,
+        recv_sem=recv,
+        device_id=device,
+        device_id_type=pl.DeviceIdType.MESH,
+    )
+
+
+def greet(devices):
+    barrier = pltpu.get_barrier_semaphore()
+    for device in devices:
+        pl.semaphore_signal(barrier, inc=1, device_id=device, device_id_type=pl.DeviceIdType.MESH)
+    return barrier
+
+
+def first_fwd(win, h, allow, rel, la, lm, qb, pb, b1, b2, gains, offs, *rest):
+    out, wa, wm, normed, qkv, probs, mixed, middle, cs, cr, rs, rr, fs, fr = rest
+    row, col = lax.axis_index("row"), lax.axis_index("col")
+    to_row, to_col = {"row": 1 - row}, {"col": 1 - col}
+    barrier = greet([to_row, to_col])
+    pl.semaphore_wait(barrier, 2)
+    blocks = [(la, wa, k) for k in range(4)]
+    for j in range(4):
+        blocks += [(lm, wm, j), (lm, wm, 4 + j)]
+    over_col, over_row, onward = [], [], []
+    for i, (src, dst, k) in enumerate(blocks):
+        over_col.append(
+            partner_copy(src.at[k], dst.at[row, col, k], cs.at[i], cr.at[i], to_col)
+        )
+        over_row.append(
+            partner_copy(src.at[k], dst.at[row, col, k], rs.at[i], rr.at[i], to_row)
+        )
+        far = dst.at[row, 1 - col, k]
+        onward.append(partner_copy(far, far, fs.at[i], fr.at[i], to_row))
+        over_col[i].start()
+        over_row[i].start()
+    wa[row, col] = la[...]
+    wm[row, col] = lm[...]
+    for i in range(4):
+        over_col[i].wait_recv()
+        onward[i].start()
+    for i in range(4):
+        over_row[i].wait_recv()
+        onward[i].wait_recv()
+    attn_fwd(win, h, allow, rel, wa, qb, pb, gains, offs, normed, qkv, probs, mixed, middle)
+    mv = middle[...]
+    x, _ = norm_parts(mv)
+    nv = (x * gains[1:2] + offs[1:2]).astype(BF)
+    acc = [mv[:, cut(r)] + b2[:, cut(r)] for r in range(2)]
+    for near in range(2):
+        c = col if near == 0 else 1 - col
+        for j in range(4):
+            for i in (4 + 2 * j, 5 + 2 * j):
+                if near == 0:
+                    over_row[i].wait_recv()
+                else:
+                    over_col[i].wait_recv()
+                    onward[i].start()
+            if near == 1:
+                onward[4 + 2 * j].wait_recv()
+                onward[5 + 2 * j].wait_recv()
+            pre = nn(nv[:, cut(0)], wm[0, c, j]) + nn(nv[:, cut(1)], wm[1, c, j]) + b1[c * 4 + j]
+            av = (pre * (0.5 + 0.5 * lax.erf(pre * (0.5 ** 0.5)))).astype(BF)
+            for r in range(2):
+                acc[r] = acc[r] + nn(av, wm[r, c, 4 + j])
+    for r in range(2):
+        out[:, cut(r)] = acc[r].astype(BF)
+    for i in range(12):
+        over_col[i].wait_send()
+        over_row[i].wait_send()
+        onward[i].wait_send()
+
+
+def reduce_grads(line, gm, ga, out, rbuf, csend, cbuf, zsum, ebuf, wsum, mbuf, *sems):
+    rs, rr, cs, cr, es, er, ms, mr, bs, br = sems
+    row, col, place = lax.axis_index("row"), lax.axis_index("col"), lax.axis_index("dp")
+    to_row, to_col = {"row": 1 - row}, {"col": 1 - col}
+    inner = (place == 1) | (place == 2)
+    outer = jnp.logical_not(inner)
+    to_pair = {"dp": place + 1 - 2 * lax.rem(place, 2)}
+    to_other = {"dp": 3 - place}
+    barrier = greet([to_row, to_col] + ([to_pair] if line else []))
+    if line:
+
+        @pl.when(inner)
+        def _():
+            greet([to_other])
+            pl.semaphore_wait(barrier, 4)
+
+        @pl.when(outer)
+        def _():
+            pl.semaphore_wait(barrier, 3)
+    else:
+        pl.semaphore_wait(barrier, 2)
+
+    def grad(k):
+        return (gm, k) if k < 8 else (ga, k - 8)
+
+    over_row, over_col = [], []
+    for k in range(12):
+        ref, at = grad(k)
+        over_row.append(
+            partner_copy(ref.at[1 - row, :, at], rbuf.at[k], rs.at[k], rr.at[k], to_row)
+        )
+        over_row[k].start()
+    for k in range(12):
+        ref, at = grad(k)
+        over_row[k].wait_recv()
+        other = ref[row, 1 - col, at].astype(F32) + rbuf[k, 1 - col].astype(F32)
+        csend[k] = other.astype(BF)
+        over_col.append(partner_copy(csend.at[k], cbuf.at[k], cs.at[k], cr.at[k], to_col))
+        over_col[k].start()
+    to_inner = [
+        partner_copy(zsum.at[k], ebuf.at[k], es.at[k], er.at[k], to_pair) for k in range(12 if line else 0)
+    ]
+    across = [
+        partner_copy(wsum.at[k], mbuf.at[k], ms.at[k], mr.at[k], to_other) for k in range(12 if line else 0)
+    ]
+    to_outer = [
+        partner_copy(out.at[k], out.at[k], bs.at[k], br.at[k], to_pair) for k in range(12 if line else 0)
+    ]
+    for t in range(14 if line else 12):
+        if t < 12:
+            ref, at = grad(t)
+            over_col[t].wait_recv()
+            mine = ref[row, col, at].astype(F32) + rbuf[t, col].astype(F32)
+            total = (mine + cbuf[t].astype(F32)).astype(BF)
+            if not line:
+                out[t] = total
+                continue
+            zsum[t] = total
+
+            @pl.when(outer)
+            def _():
+                to_inner[t].start()
+
+        @pl.when(inner)
+        def _():
+            if 1 <= t < 13:
+                k = t - 1
+                to_inner[k].wait_recv()
+                wsum[k] = (zsum[k].astype(F32) + ebuf[k].astype(F32)).astype(BF)
+                across[k].start()
+            if t >= 2:
+                k = t - 2
+                across[k].wait_recv()
+                out[k] = (wsum[k].astype(F32) + mbuf[k].astype(F32)).astype(BF)
+                to_outer[k].start()
+
+    for k in range(12):
+        over_row[k].wait_send()
+        over_col[k].wait_send()
+    if line:
+
+        @pl.when(outer)
+        def _():
+            for k in range(12):
+                to_outer[k].wait_recv()
+                to_inner[k].wait_send()
+
+        @pl.when(inner)
+        def _():
+            for k in range(12):
+                across[k].wait_send()
+                to_outer[k].wait_send()
+
+
+def run(body, args, outs, name, flops, scratch=(), shared=None):
     shapes = [jax.ShapeDtypeStruct(s, d) for s, d in outs]
     moved = sum(a.size * a.dtype.itemsize for a in list(args) + shapes)
     vm = pl.BlockSpec(memory_space=pltpu.VMEM)
@@ -216,7 +386,11 @@
         in_specs=[vm] * len(args),
         out_specs=[vm] * len(outs),
         scratch_shapes=list(scratch),
-        compiler_params=pltpu.CompilerParams(vmem_limit_bytes=48 * 1024 * 1024),
+        compiler_params=pltpu.CompilerParams(
+            vmem_limit_bytes=48 * 1024 * 1024,
+            collective_id=shared,
+            has_side_effects=shared is not None,
+        ),
         cost_estimate=pl.CostEstimate(flops=flops, bytes_accessed=moved, transcendentals=0),
         name=name,
     )(*args)
@@ -295,17 +469,14 @@
         [fc1_weight[0].reshape(B, 4, B).transpose(1, 0, 2), fc2_weight[0].reshape(4, B, B)], axis=0
     )
 
-    def gather_weights(x):
-        x = lax.all_gather(x, "col", axis=0)
-        return lax.all_gather(x, "row", axis=0)
-
-    attn_w = gather_weights(attn_w)
-    mlp_w = gather_weights(mlp_w)
     zeros = jnp.zeros_like(qkv_bias[0, 0])
     packed = jnp.concatenate(
         [qkv_bias[0, 0], zeros, qkv_bias[0, 1], fc1_bias[0], bias_table[0].T.reshape(-1)]
     )
-    packed = lax.all_gather(packed, "col", axis=0)
+    packed_other = swap(packed, "col")
+    packed = jnp.where(
+        col == 0, jnp.stack([packed, packed_other]), jnp.stack([packed_other, packed])
+    )
     qb = packed[:, :768]
     b1 = packed[:, 768:1792].reshape(1, FF)
     table = packed[:, 1792:].reshape(HEADS, TABLE)
@@ -372,7 +543,36 @@
         return res[1:], res2[1:], from_win(res2[0])
 
     both = ("pipe", "col")
-    _, nat = forward(to_win(images))
+    dma = pltpu.SemaphoreType.DMA((12,))
+    out_first, attn_w, mlp_w = run(
+        lambda *a: first_fwd(win, *a),
+        (
+            to_win(images),
+            allow,
+            rel,
+            attn_w,
+            mlp_w,
+            qb,
+            pb,
+            b1.reshape(8, 1, B),
+            b2,
+            gains,
+            offs,
+        ),
+        [((rows, D), BF), ((2, 2, 4, B, B), BF), ((2, 2, 8, B, B), BF)],
+        "first_fwd",
+        2 * rows * D * (4 * D + 2 * FF),
+        [
+            pltpu.VMEM((rows, D), BF),
+            pltpu.VMEM((2, rows, 768), BF),
+            pltpu.VMEM((win * 4, 4 * PAD, PAD), F32),
+            pltpu.VMEM((rows, D), BF),
+            pltpu.VMEM((rows, D), F32),
+        ]
+        + [dma] * 6,
+        0,
+    )
+    nat = from_win(out_first)
     kept_part = lax.ppermute(nat[:, 98 - KEPT :], both, [(0, 2), (1, 3)])
     sent_part = lax.ppermute(nat[:, : 98 - KEPT], both, [(0, 3), (1, 2)])
     received = jnp.concatenate([kept_part, sent_part], axis=1)
@@ -393,17 +593,21 @@
     layer_outputs = unroll(nat_out)[None]
     input_grads = unroll(g_in)[None]
 
-    def reduce_grads(x):
-        mine = lax.dynamic_index_in_dim(x, row, 0, keepdims=False)
-        other = lax.dynamic_index_in_dim(x, 1 - row, 0, keepdims=False)
-        y = mine.astype(F32) + swap(other, "row").astype(F32)
-        mine = lax.dynamic_index_in_dim(y, col, 0, keepdims=False)
-        other = lax.dynamic_index_in_dim(y, 1 - col, 0, keepdims=False).astype(BF)
-        z = mine + swap(other, "col").astype(F32)
-        return lax.psum(z.astype(BF), "dp").astype(F32)
-
-    g_mlp = reduce_grads(mlp_res[0])
-    g_attn = reduce_grads(attn_res[0])
+    line = lax.axis_size("dp") == 4
+    block = pltpu.VMEM((12, B, B), BF)
+    (grads,) = run(
+        lambda *a: reduce_grads(line, *a),
+        (mlp_res[0], attn_res[0]),
+        [((12, B, B), BF)],
+        "reduce_grads",
+        12 * B * B * 16,
+        [pltpu.VMEM((12, 2, B, B), BF)] + [block] * 6 + [dma] * 10,
+        1,
+    )
+    if not line:
+        grads = lax.psum(grads, "dp")
+    grads = grads.astype(F32)
+    g_mlp, g_attn = grads[:8], grads[8:]
     table_part = lax.dot_general(
         attn_res[3].reshape(HEADS, PAD * PAD),
         onehot,

time: 317 us -> 275 us (0.87)
  waiting for transfers between devices: 105 us -> 5.96 us
  Pallas kernels: 48.9 us -> 134 us
  between operations: 15.5 us -> 1.53 us
  blocking collectives: 72.1 us -> 59.4 us
  other arithmetic: 19.5 us -> 9.17 us
  local copies, waits for them, and re-layouts: 35.7 us -> 44.8 us
    pallas_call x8, Pallas kernels: 48.9 us -> 134 us  [run(): pl.pallas_call(body, out_shape=shapes, in_specs=[vm] * len(args), out_spe...]
    all_gather x4 -> x0, waiting for transfers between devices: 66.1 us -> none  [the longest x2 57.1 us: gather_weights(): x = lax.all_gather(x, 'col', axis=0)]
    ppermute x7 -> x4, waiting for transfers between devices: 29.8 us -> 0.01 us  [swap(): return lax.ppermute(x, axis, [(0, 1), (1, 0)])]
    unnamed x124 -> x107, local copies, waits for them, and re-layouts: 9.82 us -> 23.2 us
    unnamed x1 -> x0, blocking collectives: 8.64 us -> none
    add x2 -> x0, other arithmetic: 5.62 us -> none  [reduce_grads(): y = mine.astype(F32) + swap(other, 'row').astype(F32)]
    convert_element_type x4 -> x1, other arithmetic: 6.43 us -> 1.92 us  [per_device(): grads = grads.astype(F32)]
    squeeze x2 -> x0, local copies, waits for them, and re-layouts: 4.4 us -> none  [reduce_grads(): other = lax.dynamic_index_in_dim(x, 1 - row, 0, keepdims=False)]
  transfers between devices with their start and end apart: 16 -> 8, of which waited for: 9 -> 2; matrix products, arithmetic and copies ran while one was open for 10% -> 9% of each run, Pallas kernels for 4% -> 19%
where the time goes in v2:
time: 275 us; the launch traced here: 274 us
  Pallas kernels  134 us (49%)
  blocking collectives  59.4 us (22%)
  local copies, waits for them, and re-layouts  44.8 us (16%)
  starting transfers between devices  12 us (4%)
  other arithmetic  9.17 us (3%)
  matrix products  7.28 us (3%)
  waiting for transfers between devices  5.96 us (2%)
    pallas_call x8, Pallas kernels, run(): pl.pallas_call(body, out_shape=shapes, in_specs=[vm] * len(args), out_spe...  134 us
    psum x1, blocking collectives, per_device(): flat = lax.psum(flat, ('dp', 'row', 'col'))  59.4 us
    unnamed x107, local copies, waits for them, and re-layouts  23.2 us
  transfers between devices with their start and end apart: 8, of which 2 were waited for; matrix products, arithmetic and copies ran while one was open for 9% of the time, Pallas kernels for 19%

profile of v2, /device:TPU:0, one launch (start us, length us, event | category | flops | bytes accessed | tf_op | source)
XLA Modules:
  0.0 273.9 jit_solution(8815617501356391400)
XLA Ops:
  3.0 3.0 %collective-permute-start = (f32[3144]{0:T(1024)S(1)}, f32[3144]{0:T(1024)S(1)}, u32[]{:S(2)}, u32[]{:S(2)}) collective-permute-start(f32[3144]{0:T(1024)S(1)} %constant_dynamic-update-slice_fusion.2), channel_id=1, source_target_pairs={{0,1},{1,0},{2,3},{3,2},{4,5},{5,4},{6,7},{7,6},{8,9},{9,8},{10,11... | collective-permute-start | bytes 37736 | tf_op jit(solution)/shard_map/ppermute | solution.py:463
  6.0 1.6 slice.145
  10.2 1.2 copy.42
  16.3 41.0 %first_fwd.1 = (bf16[256,512]{1,0:T(8,128)(2,1)S(1)}, bf16[2,2,4,256,256]{4,3,2,1,0:T(8,128)(2,1)S(1)}, bf16[2,2,8,256,256]{4,3,2,1,0:T(8,128)(2,1)}) custom-call(bf16[256,512]{1,0:T(8,128)(2,1)S(1)} %convolution_convert_fusion.3.a_0_, f32[4,256,64]{2,1,0:T(8,128)S(1)} %bitcast.64, f32[4,256,64]{2,1,0:T(8,128)S(1)} %reshape.367.a_2_, ...), custom_call_target="tpu_custom_call" | custom-call | flops 1610612736 | bytes 8939520 | tf_op jit(solution)/shard_map/first_fwd/pallas_call | solution.py:383
  57.3 1.3 copy-done
  59.0 3.1 %collective-permute-start.2 = (bf16[2,42,512]{2,1,0:T(8,128)(2,1)S(1)}, bf16[2,42,512]{2,1,0:T(8,128)(2,1)S(1)}, u32[]{:S(2)}, u32[]{:S(2)}) collective-permute-start(bf16[2,42,512]{2,1,0:T(8,128)(2,1)S(1)} %slice.175), channel_id=1, source_target_pairs={{0,17},{1,16},{2,19},{3,18},{4,21},{5,20},{6,23},{7,22},{8,25},{9,... | collective-permute-start | bytes 258056 | tf_op jit(solution)/shard_map/ppermute | solution.py:577
  62.1 1.5 collective-permute-start.1
  65.8 1.8 collective-permute-done.1
  69.0 4.0 %attn_fwd.1 = (bf16[256,512]{1,0:T(8,128)(2,1)S(1)}, bf16[2,256,768]{2,1,0:T(8,128)(2,1)S(1)}, f32[16,256,64]{2,1,0:T(8,128)S(1)}, bf16[256,512]{1,0:T(8,128)(2,1)S(1)}, f32[256,512]{1,0:T(8,128)S(1)}) custom-call(bf16[256,512]{1,0:T(8,128)(2,1)S(1)} %convolution_convert_fusion.2.a_0_.a_5_, f32[4,256,64]{2,1,0:T(8,128)S(1)} %bitcast.65, ...), custom_call_target="tpu_custom_call" | custom-call | flops 536870912 | bytes 5783552 | tf_op jit(solution)/shard_map/attn_fwd/pallas_call | solution.py:383
  75.3 4.7 %mlp_fwd.1 = (bf16[256,512]{1,0:T(8,128)(2,1)S(1)}, bf16[256,2048]{1,0:T(8,128)(2,1)S(1)}, f32[256,2048]{1,0:T(8,128)S(1)}, bf16[256,512]{1,0:T(8,128)(2,1)S(1)}) custom-call(f32[256,512]{1,0:T(8,128)S(1)} %get-tuple-element.36.middle.a_4_, bf16[2,2,8,256,256]{4,3,2,1,0:T(8,128)(2,1)} %get-tuple-element.37.w.a_5_, f32[1,2048]{1,0:T(1,128)S(1)} %bitcast.73, ...), custom_call_target="tpu_custom_call" | custom-call | flops 1073741824 | bytes 8407040 | tf_op jit(solution)/shard_map/mlp_fwd/pallas_call | solution.py:383
  80.0 1.4 copy-done.2
  85.6 1.5 collective-permute-start.3
  87.1 1.6 copy-done.3
  90.9 4.6 %mlp_bwd.2.a_0_ = f32[256,512]{1,0:T(8,128)S(1)} custom-call(bf16[256,512]{1,0:T(8,128)(2,1)S(1)} %copy-done.15, bf16[256,2048]{1,0:T(8,128)(2,1)S(1)} %copy-done.6, f32[256,2048]{1,0:T(8,128)S(1)} %copy-done.3, bf16[256,512]{1,0:T(8,128)(2,1)S(1)} %copy-done.22, f32[256,512]{1,0:T(8,128)S(1)} %get-tuple-element.36.middle.a_4_, ...), custom_call_target="tpu_custom_call" | custom-call | flops 1073741824 | bytes 8916992 | tf_op jit(solution)/shard_map/mlp_bwd/pallas_call | solution.py:383
  95.6 7.3 %attn_bwd.2 = bf16[256,512]{1,0:T(8,128)(2,1)S(1)} custom-call(f32[256,512]{1,0:T(8,128)S(1)} %mlp_bwd.2.a_0_, bf16[256,512]{1,0:T(8,128)(2,1)S(1)} %copy-done.19, bf16[2,256,768]{2,1,0:T(8,128)(2,1)S(1)} %copy-done.9, f32[16,256,64]{2,1,0:T(8,128)S(1)} %get-tuple-element.44.a_3_, bf16[256,512]{1,0:T(8,128)(2,1)S(1)} %copy-done.17, ...), custom_call_target="tpu_custom_call" | custom-call | flops 1073741824 | bytes 5509120 | tf_op jit(solution)/shard_map/attn_bwd/pallas_call | solution.py:383
  104.0 1.7 reshape.371
  105.6 1.7 reshape.374
  109.1 1.3 collective-permute-start.6
  110.4 1.5 collective-permute-start.5
  113.8 4.1 %collective-permute-done.5 = bf16[2,42,512]{2,1,0:T(8,128)(2,1)S(1)} collective-permute-done((bf16[2,42,512]{2,1,0:T(8,128)(2,1)S(1)}, bf16[2,42,512]{2,1,0:T(8,128)(2,1)S(1)}, u32[]{:S(2)}, u32[]{:S(2)}) %collective-permute-start.5) | collective-permute-done | bytes 86048 | tf_op jit(solution)/shard_map/ppermute | solution.py:585
  118.7 1.7 concatenate.60
  123.7 7.7 %mlp_bwd.3 = (f32[256,512]{1,0:T(8,128)S(1)}, bf16[2,2,8,256,256]{4,3,2,1,0:T(8,128)(2,1)}, f32[1,2048]{1,0:T(1,128)S(1)}, f32[3,512]{1,0:T(4,128)S(1)}) custom-call(bf16[256,512]{1,0:T(8,128)(2,1)S(1)} %convolution_convert_fusion.a_0_, bf16[256,2048]{1,0:T(8,128)(2,1)S(1)} %copy-done.7, f32[256,2048]{1,0:T(8,128)S(1)} %copy-done.4, ...), custom_call_target="tpu_custom_call" | custom-call | flops 2147483648 | bytes 13125632 | tf_op jit(solution)/shard_map/mlp_bwd/pallas_call | solution.py:383
  131.4 8.4 %attn_bwd.3 = (bf16[256,512]{1,0:T(8,128)(2,1)S(1)}, bf16[2,2,4,256,256]{4,3,2,1,0:T(8,128)(2,1)S(1)}, f32[2,768]{1,0:T(2,128)S(1)}, f32[3,512]{1,0:T(4,128)S(1)}, f32[4,256,64]{2,1,0:T(8,128)S(1)}) custom-call(f32[256,512]{1,0:T(8,128)S(1)} %get-tuple-element.46.a_0_, bf16[256,512]{1,0:T(8,128)(2,1)S(1)} %copy-done.20, bf16[2,256,768]{2,1,0:T(8,128)(2,1)S(1)} %copy-done.10, ...), custom_call_target="tpu_custom_call" | custom-call | flops 1073741824 | bytes 7880704 | tf_op jit(solution)/shard_map/attn_bwd/pallas_call | solution.py:383
  139.9 1.3 copy-done.13
  141.6 1.6 copy-done.14
  143.2 55.9 %reduce_grads.1 = bf16[12,256,256]{2,1,0:T(8,128)(2,1)S(1)} custom-call(bf16[2,2,8,256,256]{4,3,2,1,0:T(8,128)(2,1)} %get-tuple-element.48.a_0_, bf16[2,2,4,256,256]{4,3,2,1,0:T(8,128)(2,1)S(1)} %copy-done.14), custom_call_target="tpu_custom_call" | custom-call | flops 12582912 | bytes 7864320 | tf_op jit(solution)/shard_map/reduce_grads/pallas_call | solution.py:383
  199.1 1.9 convert_element_type.72
  202.0 1.4 fusion
  203.6 59.4 %psum.7 = f32[9360]{0:T(1024)S(1)} all-reduce(f32[9360]{0:T(1024)S(1)} %constant_dynamic-update-slice_fusion.5), channel_id=1, replica_groups=mesh['pipe'=2,'dp'=4,'row'=2,'col'=2] {'dp','row','col'}, use_global_device_ids=true, to_apply=%region_0.1 | all-reduce | flops 9360 | bytes 74880 | tf_op jit(solution)/shard_map/psum | solution.py:619
  263.6 2.1 slice_bitcast_fusion.1
  265.7 1.3 slice_bitcast_fusion
  268.5 1.3 copy.50
  (195 shorter events, 38.4 us)
Async XLA Ops:
  0.6 12.0 %copy-start.28 = (bf16[256,196]{1,0:T(8,128)(2,1)S(1)}, bf16[256,196]{1,0:T(8,128)(2,1)}, u32[]{:S(2)}) copy-start(bf16[256,196]{1,0:T(8,128)(2,1)} %constant.56.clone) | copy-start | bytes 301060
  0.7 12.0 %copy-start.32 = (bf16[256,196]{1,0:T(8,128)(2,1)S(1)}, bf16[256,196]{1,0:T(8,128)(2,1)}, u32[]{:S(2)}) copy-start(bf16[256,196]{1,0:T(8,128)(2,1)} %constant.57.clone) | copy-start | bytes 301060
  0.7 11.1 %copy-start.41 = (bf16[1,1024,256]{2,1,0:T(8,128)(2,1)S(1)}, bf16[1,1024,256]{2,1,0:T(8,128)(2,1)}, u32[]{:S(2)}) copy-start(bf16[1,1024,256]{2,1,0:T(8,128)(2,1)} %param.26) | copy-start | bytes 1572868
  3.0 11.1 %collective-permute-start = (f32[3144]{0:T(1024)S(1)}, f32[3144]{0:T(1024)S(1)}, u32[]{:S(2)}, u32[]{:S(2)}) collective-permute-start(f32[3144]{0:T(1024)S(1)} %constant_dynamic-update-slice_fusion.2), channel_id=1, source_target_pairs={{0,1},{1,0},{2,3},{3,2},{4,5},{5,4},{6,7},{7,6},{8,9},{9,8},{10,11... | collective-permute-start | bytes 37736 | tf_op jit(solution)/shard_map/ppermute | solution.py:463
  7.6 56.0 %collective-permute-start.4 = (bf16[2,42,512]{2,0,1:T(2,128)(2,1)}, bf16[2,42,512]{2,0,1:T(2,128)(2,1)}, u32[]{:S(2)}, u32[]{:S(2)}) collective-permute-start(bf16[2,42,512]{2,0,1:T(2,128)(2,1)} %slice.145), channel_id=1, source_target_pairs={{0,1},{1,0},{2,3},{3,2},{4,5},{5,4},{6,7},{7,6},{8,9},{9,8},{10,11... | collective-permute-start | bytes 258056 | tf_op jit(solution)/shard_map/ppermute | solution.py:463
  11.7 4.5 %copy-start.24 = (f32[1,2,512]{2,1,0:T(2,128)S(1)}, f32[1,2,512]{2,1,0:T(2,128)}, u32[]{:S(2)}) copy-start(f32[1,2,512]{2,1,0:T(2,128)} %param.28) | copy-start | bytes 12292
  16.1 41.2 %copy-start.11 = (f32[4,256,64]{2,1,0:T(8,128)}, f32[4,256,64]{2,1,0:T(8,128)S(1)}, u32[]{:S(2)}) copy-start(f32[4,256,64]{2,1,0:T(8,128)S(1)} %reshape.367.a_2_) | copy-start | bytes 786436
  16.2 47.3 %copy-start.43 = (f32[1,1,2,1024]{3,2,1,0:T(2,128)S(1)}, f32[1,1,2,1024]{3,2,1,0:T(2,128)}, u32[]{:S(2)}) copy-start(f32[1,1,2,1024]{3,2,1,0:T(2,128)} %get-tuple-element.76) | copy-start | bytes 24580
  16.2 47.4 %slice-start = ((bf16[2,98,512]{2,0,1:T(2,128)(2,1)}), bf16[2,56,512]{2,0,1:T(2,128)(2,1)S(1)}, s32[]{:S(2)}) async-start(bf16[2,98,512]{2,0,1:T(2,128)(2,1)} %param.19), calls=%async_computation | async-start | bytes 229376 | tf_op jit(solution)/shard_map/slice | solution.py:582
  58.6 9.0 %copy-start.39 = (bf16[2,98,512]{2,0,1:T(2,128)(2,1)S(1)}, bf16[2,98,512]{2,0,1:T(2,128)(2,1)}, u32[]{:S(2)}) copy-start(bf16[2,98,512]{2,0,1:T(2,128)(2,1)} %param.17) | copy-start | bytes 602116
  59.0 6.8 %collective-permute-start.2 = (bf16[2,42,512]{2,1,0:T(8,128)(2,1)S(1)}, bf16[2,42,512]{2,1,0:T(8,128)(2,1)S(1)}, u32[]{:S(2)}, u32[]{:S(2)}) collective-permute-start(bf16[2,42,512]{2,1,0:T(8,128)(2,1)S(1)} %slice.175), channel_id=1, source_target_pairs={{0,17},{1,16},{2,19},{3,18},{4,21},{5,20},{6,23},{7,22},{8,25},{9,... | collective-permute-start | bytes 258056 | tf_op jit(solution)/shard_map/ppermute | solution.py:577
  62.1 5.6 %collective-permute-start.1 = (bf16[2,56,512]{2,1,0:T(8,128)(2,1)S(1)}, bf16[2,56,512]{2,1,0:T(8,128)(2,1)S(1)}, u32[]{:S(2)}, u32[]{:S(2)}) collective-permute-start(bf16[2,56,512]{2,1,0:T(8,128)(2,1)S(1)} %slice.174), channel_id=1, source_target_pairs={{0,16},{1,17},{2,18},{3,19},{4,20},{5,21},{6,22},{7,23},{8,24},{9,... | collective-permute-start | bytes 344072 | tf_op jit(solution)/shard_map/ppermute | solution.py:576
  75.3 20.2 %copy-start.1 = (f32[16,256,64]{2,1,0:T(8,128)}, f32[16,256,64]{2,1,0:T(8,128)S(1)}, u32[]{:S(2)}) copy-start(f32[16,256,64]{2,1,0:T(8,128)S(1)} %get-tuple-element.44.a_3_) | copy-start | bytes 3145732
  75.3 7.7 %copy-start.29 = (bf16[256,196]{1,0:T(8,128)(2,1)S(1)}, bf16[256,196]{1,0:T(8,128)(2,1)}, u32[]{:S(2)}) copy-start(bf16[256,196]{1,0:T(8,128)(2,1)} %constant.56.clone) | copy-start | bytes 301060
  75.3 7.7 %copy-start.33 = (bf16[256,196]{1,0:T(8,128)(2,1)S(1)}, bf16[256,196]{1,0:T(8,128)(2,1)}, u32[]{:S(2)}) copy-start(bf16[256,196]{1,0:T(8,128)(2,1)} %constant.57.clone) | copy-start | bytes 301060
  75.3 11.8 %copy-start.15 = (bf16[256,512]{1,0:T(8,128)(2,1)S(1)}, bf16[256,512]{1,0:T(8,128)(2,1)}, u32[]{:S(2)}) copy-start(bf16[256,512]{1,0:T(8,128)(2,1)} %convolution_convert_fusion.1.a_0_) | copy-start | bytes 786436
  85.6 26.3 %collective-permute-start.3 = (bf16[2,42,512]{2,1,0:T(8,128)(2,1)}, bf16[2,42,512]{2,1,0:T(8,128)(2,1)}, u32[]{:S(2)}, u32[]{:S(2)}) collective-permute-start(bf16[2,42,512]{2,1,0:T(8,128)(2,1)} %slice.176), channel_id=1, source_target_pairs={{0,1},{1,0},{2,3},{3,2},{4,5},{5,4},{6,7},{7,6},{8,9},{9,8},{10,11... | collective-permute-start | bytes 258056 | tf_op jit(solution)/shard_map/ppermute | solution.py:463
  90.9 4.7 %copy-start.9 = (bf16[2,256,768]{2,1,0:T(8,128)(2,1)S(1)}, bf16[2,256,768]{2,1,0:T(8,128)(2,1)}, u32[]{:S(2)}) copy-start(bf16[2,256,768]{2,1,0:T(8,128)(2,1)} %copy-done.8) | copy-start | bytes 2359300
  90.9 4.7 %copy-start.17 = (bf16[256,512]{1,0:T(8,128)(2,1)S(1)}, bf16[256,512]{1,0:T(8,128)(2,1)}, u32[]{:S(2)}) copy-start(bf16[256,512]{1,0:T(8,128)(2,1)} %copy-done.16) | copy-start | bytes 786436
  90.9 4.7 %copy-start.19 = (bf16[256,512]{1,0:T(8,128)(2,1)S(1)}, bf16[256,512]{1,0:T(8,128)(2,1)}, u32[]{:S(2)}) copy-start(bf16[256,512]{1,0:T(8,128)(2,1)} %copy-done.18) | copy-start | bytes 786436
  95.6 7.4 %copy-start.30 = (bf16[256,196]{1,0:T(8,128)(2,1)S(1)}, bf16[256,196]{1,0:T(8,128)(2,1)}, u32[]{:S(2)}) copy-start(bf16[256,196]{1,0:T(8,128)(2,1)} %constant.56.clone) | copy-start | bytes 301060
  95.6 7.4 %copy-start.34 = (bf16[256,196]{1,0:T(8,128)(2,1)S(1)}, bf16[256,196]{1,0:T(8,128)(2,1)}, u32[]{:S(2)}) copy-start(bf16[256,196]{1,0:T(8,128)(2,1)} %constant.57.clone) | copy-start | bytes 301060
  95.6 8.3 %copy-start.38 = (bf16[2,98,512]{2,1,0:T(8,128)(2,1)S(1)}, bf16[2,98,512]{2,1,0:T(8,128)(2,1)}, u32[]{:S(2)}) copy-start(bf16[2,98,512]{2,1,0:T(8,128)(2,1)} %copy-done.37) | copy-start | bytes 602116
  103.0 18.5 %copy-start.4 = (f32[256,2048]{1,0:T(8,128)S(1)}, f32[256,2048]{1,0:T(8,128)}, u32[]{:S(2)}) copy-start(f32[256,2048]{1,0:T(8,128)} %copy-done.2) | copy-start | bytes 6291460
  109.1 8.9 %collective-permute-start.6 = (bf16[2,56,512]{2,1,0:T(8,128)(2,1)S(1)}, bf16[2,56,512]{2,1,0:T(8,128)(2,1)S(1)}, u32[]{:S(2)}, u32[]{:S(2)}) collective-permute-start(bf16[2,56,512]{2,1,0:T(8,128)(2,1)S(1)} %slice.179), channel_id=1, source_target_pairs={{16,0},{17,1},{18,2},{19,3},{20,4},{21,5},{22,6},{23,7},{24,8},{25... | collective-permute-start | bytes 344072 | tf_op jit(solution)/shard_map/ppermute | solution.py:584
  110.4 7.6 %collective-permute-start.5 = (bf16[2,42,512]{2,1,0:T(8,128)(2,1)S(1)}, bf16[2,42,512]{2,1,0:T(8,128)(2,1)S(1)}, u32[]{:S(2)}, u32[]{:S(2)}) collective-permute-start(bf16[2,42,512]{2,1,0:T(8,128)(2,1)S(1)} %slice.178), channel_id=1, source_target_pairs={{16,1},{17,0},{18,3},{19,2},{20,5},{21,4},{22,7},{23,6},{24,9},{25... | collective-permute-start | bytes 258056 | tf_op jit(solution)/shard_map/ppermute | solution.py:585
  123.7 7.7 %copy-start.10 = (bf16[2,256,768]{2,1,0:T(8,128)(2,1)S(1)}, bf16[2,256,768]{2,1,0:T(8,128)(2,1)}, u32[]{:S(2)}) copy-start(bf16[2,256,768]{2,1,0:T(8,128)(2,1)} %copy-done.8) | copy-start | bytes 2359300
  123.7 7.7 %copy-start.20 = (bf16[256,512]{1,0:T(8,128)(2,1)S(1)}, bf16[256,512]{1,0:T(8,128)(2,1)}, u32[]{:S(2)}) copy-start(bf16[256,512]{1,0:T(8,128)(2,1)} %copy-done.18) | copy-start | bytes 786436
  131.4 9.8 %copy-start.31 = (bf16[256,196]{1,0:T(8,128)(2,1)S(1)}, bf16[256,196]{1,0:T(8,128)(2,1)}, u32[]{:S(2)}) copy-start(bf16[256,196]{1,0:T(8,128)(2,1)} %constant.56.clone) | copy-start | bytes 301060
  131.4 9.8 %copy-start.35 = (bf16[256,196]{1,0:T(8,128)(2,1)S(1)}, bf16[256,196]{1,0:T(8,128)(2,1)}, u32[]{:S(2)}) copy-start(bf16[256,196]{1,0:T(8,128)(2,1)} %constant.57.clone) | copy-start | bytes 301060
  263.0 5.0 %copy-start.42 = (f32[9360]{0:T(1024)}, f32[9360]{0:T(1024)S(1)}, u32[]{:S(2)}) copy-start(f32[9360]{0:T(1024)S(1)} %psum.7) | copy-start | bytes 112324
  268.0 4.9 %collective-permute-start.7 = (bf16[2,42,512]{2,1,0:T(8,128)(2,1)S(1)}, bf16[2,42,512]{2,1,0:T(8,128)(2,1)S(1)}, u32[]{:S(2)}, u32[]{:S(2)}) collective-permute-start(bf16[2,42,512]{2,1,0:T(8,128)(2,1)S(1)} %slice.180), channel_id=1, source_target_pairs={{0,1},{1,0},{2,3},{3,2},{4,5},{5,4},{6,7},{7,6},{8,9},{9,8},{10,11... | collective-permute-start | bytes 258056 | tf_op jit(solution)/shard_map/ppermute | solution.py:463
  (24 other events, 46.3 us)
